TPU v7x, 32 devices: a whole 2x2x4 slice. The times are simulated.
32 devices in a mesh: dp: 8 (over z, y), tensor: 4 (over x, core).
Axes of the slice: x: 2, y: 2, z: 4, core: 2. Of those that a mesh axis runs over, the one named last changes fastest.
Arguments:
- input_token_ids: int32 [4, 32, 512], P(None, ('dp', 'tensor')), may hold values from 0 to 50264
- segments: int32 [4, 32, 512], P(None, ('dp', 'tensor')), may hold values from -1 to 63, as said below
- labels: float32 [4, 32, 64], P(None, ('dp', 'tensor')), may hold values from 0 to 5
- embedding: bfloat16 [768, 50265], P('tensor'), may hold values from -6 to 6
- position_embedding_table: bfloat16 [512, 768], replicated, may hold values from -3 to 3
- norm_gain_rows: float32 [3, 768], replicated, may hold values from 0.5 to 1.5
- norm_shift_rows: float32 [3, 768], replicated, may hold values from -0.3 to 0.3
- query_key_value_weight: bfloat16 [3, 768, 768], replicated, may hold values from -0.21875 to 0.21875
- attention_output_weight: bfloat16 [768, 768], replicated, may hold values from -0.625 to 0.625
- attention_bias_stack: float32 [5, 768], replicated, may hold values from -0.3 to 0.3
- feedforward_in_weight: bfloat16 [768, 3072], P(None, 'tensor'), may hold values from -0.21875 to 0.21875
- feedforward_bias: bfloat16 [3072], P('tensor'), may hold values from -0.59765625 to 0.59765625
- feedforward_out_weight: bfloat16 [3072, 768], P('tensor'), may hold values from -0.109375 to 0.109375
- adapter_down_weight: bfloat16 [2, 768, 8], replicated, may hold values from -0.21875 to 0.21875
- adapter_up_weight: float32 [2, 8, 768], replicated, may hold values from -0.3 to 0.3
- adapter_momentum: float32 [2, 8, 768], replicated, may hold values from -0.0017089844 to 0.0017089844
- head: float32 [769], replicated, may hold values from -0.21875 to 0.21875
- head_first_moment: float32 [769], replicated, may hold values from -0.015625 to 0.015625
- head_second_moment: float32 [769], replicated, may hold values from 6e-08 to 2.6e-07
Outputs:
- squared_error_sum: float32 [], replicated
- item_count: float32 [], replicated
- global_gradient_norm: float32 [], replicated
- adapter_moment_next: float32 [2, 8, 768], replicated
- adapter_up_updated: float32 [2, 8, 768], replicated
- lora_low: bfloat16 [2, 8, 768], replicated
- head_moment_next: float32 [769], replicated
- head_square_next: float32 [769], replicated
- head_updated: float32 [769], replicated
- head_low: bfloat16 [769], replicated
Inputs may be any that keep to these rules, and one draw needn't show every extreme that they name: `segments`: each sequence holds whole items from its first row on, numbered 0, 1, 2, ... in order, each of 8 to 128 rows; the rows after the last item are -1. In the first micro-batch one sequence is filled entirely with items of 8 rows, so item numbers reach 63.
All inputs are finite; a program needn't handle non-finite values.
Results may differ from a plain program's by a relative error of at most 0.0055.
Values may be sent and summed in bfloat16 or wider, within the bound.
No kernel may reach another device: no remote copies, remote signals or barrier semaphores. Data moves between devices by JAX's collectives and lax.ppermute only.
A program may use at most 320 MiB of HBM per device.

v0:
```python
import functools
import math

import jax
import jax.numpy as jnp
from jax import lax
from jax.experimental import pallas as pl
from jax.experimental.pallas import tpu as pltpu
from jax.sharding import PartitionSpec as P

HEAD_DIM = 64
STEP = 10
LN_EPS = 1e-05
CLIP_NORM = 0.5
ORTHO_MOMENTUM = 0.5
ORTHO_STEP_SIZE = 1.0
NS_A = 3.4445
NS_B = -4.775
NS_C = 2.0315
BETA_ONE = 0.9
BETA_TWO = 0.999
ADAM_RATE = 0.05
ADAM_EPS = 1e-08
DECAY = 0.01

F32 = jnp.float32
BF16 = jnp.bfloat16
LANES = 128
GROUP = 256
PER_GROUP = GROUP // HEAD_DIM
BLOCK = 128
SPAN = 3 * BLOCK
STEP_ROWS = 64
VOCAB_BLOCK = 2048
RING = 6
UNROLL = 64
ACC_ROWS = 24
BIAS_ROWS = 16
MIB = 1024 * 1024
NN = (((1,), (0,)), ((), ()))
NT = (((1,), (1,)), ((), ()))
TN = (((0,), (0,)), ((), ()))
INV_SQRT2 = 1.0 / math.sqrt(2.0)
INV_SQRT_2PI = 1.0 / math.sqrt(2.0 * math.pi)

VMEM = pl.BlockSpec(memory_space=pltpu.VMEM)
SMEM = pl.BlockSpec(memory_space=pltpu.SMEM)
ANY = pl.BlockSpec(memory_space=pl.ANY)


def mm(left, right, dims=NN):
    return lax.dot_general(left, right, dims, preferred_element_type=F32)


def row_mean(rows):
    return jnp.mean(rows, axis=-1, keepdims=True)


def add_all(terms):
    return functools.reduce(jnp.add, terms)


def at(i):
    return pl.ds(pl.multiple_of(i * STEP_ROWS, STEP_ROWS), STEP_ROWS)


def embed_kernel(*refs, parts, units):
    ids = refs[:parts]
    table, tail = refs[parts : parts + 2]
    outs = refs[parts + 2 : parts + 2 + parts * units]
    scratch = refs[parts + 2 + parts * units :]
    feats = table.shape[0]
    full = table.shape[1] // VOCAB_BLOCK
    lanes = [(lo, min(lo + LANES, feats)) for lo in range(0, feats, LANES)]
    turned = scratch[: len(lanes)]
    picked = scratch[len(lanes) : 2 * len(lanes)]
    ring, stage, ring_sems, sems = scratch[2 * len(lanes) :]

    def fetch(i):
        cols = pl.ds(pl.multiple_of(i * VOCAB_BLOCK, VOCAB_BLOCK), VOCAB_BLOCK)
        slot = lax.rem(i, RING)
        return pltpu.make_async_copy(table.at[:, cols], ring.at[slot], ring_sems.at[slot])

    def turn_block(base, block):
        for c in range(0, VOCAB_BLOCK, GROUP):
            rows_at = pl.ds(pl.multiple_of(base + c, GROUP), GROUP)
            for (lo, hi), turn in zip(lanes, turned):
                turn[rows_at, :] = block[lo:hi, c : c + GROUP].T.astype(F32)

    for i in range(min(RING, full)):
        fetch(i).start()
    turn_block(full * VOCAB_BLOCK, tail)

    def step(i, carry):
        fetch(i).wait()
        turn_block(i * VOCAB_BLOCK, ring.at[lax.rem(i, RING)])

        @pl.when(i + RING < full)
        def _():
            fetch(i + RING).start()

        return carry

    lax.fori_loop(0, full, step, 0)

    length = stage.shape[1]
    copies = []
    for p, out in enumerate(outs):
        u, r = p // parts, p % parts
        slot = p % 2

        def rows(i, carry, u=u, r=r):
            top = pl.multiple_of(i * UNROLL, UNROLL)
            for j in range(UNROLL):
                token = ids[r][u, 0, top + j]
                for turn, pick in zip(turned, picked):
                    pick[pl.ds(top + j, 1), :] = turn[pl.ds(token, 1), :]
            return carry

        lax.fori_loop(0, length // UNROLL, rows, 0)
        if p >= 2:
            copies[p - 2].wait()
        for (lo, hi), pick in zip(lanes, picked):
            stage[slot, :, lo:hi] = pick[...].astype(BF16)
        copies.append(pltpu.make_async_copy(stage.at[slot], out, sems.at[slot]))
        copies[p].start()
    for copy in copies[-2:]:
        copy.wait()


def embed_call(ids, table):
    parts = len(ids)
    units, _, length = ids[0].shape
    feats, vocab = table.shape
    full = vocab // VOCAB_BLOCK
    widths = [min(LANES, feats - lo) for lo in range(0, feats, LANES)]
    scratch = [pltpu.VMEM(((full + 1) * VOCAB_BLOCK, w), F32) for w in widths]
    scratch += [pltpu.VMEM((length, w), F32) for w in widths]
    scratch += [
        pltpu.VMEM((RING, feats, VOCAB_BLOCK), BF16),
        pltpu.VMEM((2, length, feats), BF16),
        pltpu.SemaphoreType.DMA((RING,)),
        pltpu.SemaphoreType.DMA((2,)),
    ]
    last = pl.cdiv(vocab, VOCAB_BLOCK) - 1
    tail = pl.BlockSpec((feats, VOCAB_BLOCK), lambda i: (0, last), pipeline_mode=pl.Buffered(1))
    return pl.pallas_call(
        functools.partial(embed_kernel, parts=parts, units=units),
        grid=(1,),
        in_specs=[SMEM] * parts + [ANY, tail],
        out_specs=[ANY] * (parts * units),
        out_shape=[jax.ShapeDtypeStruct((length, feats), BF16)] * (parts * units),
        scratch_shapes=scratch,
        compiler_params=pltpu.CompilerParams(vmem_limit_bytes=62 * MIB),
        name="embed",
    )(*ids, table, table)


def interleave(*lists):
    done = [0] * len(lists)
    while any(n < len(steps) for n, steps in zip(done, lists)):
        share = [n / len(steps) if steps else 1.0 for n, steps in zip(done, lists)]
        i = share.index(min(share))
        lists[i][done[i]]()
        done[i] += 1


def tile_rows(t, rows):
    lo = min(max(2 * t - 1, 0) * BLOCK, rows - min(SPAN, rows))
    return lo, min((2 * t + 3) * BLOCK, rows)


def block_pieces(b, blocks):
    first, last = max(b - 1, 0), min(b + 1, blocks - 1)
    found = []
    for t in range(blocks * BLOCK // GROUP):
        lo, hi = max(first, 2 * t), min(last, 2 * t + 1)
        if lo <= hi:
            found.append((t, lo, hi))
    return found


def spread(values, t, lo, hi):
    zero_block = jnp.zeros((BLOCK, BLOCK), BF16)
    parts = [values] if lo == 2 * t else [zero_block, values]
    if hi == 2 * t:
        parts.append(zero_block)
    return parts[0] if len(parts) == 1 else jnp.concatenate(parts, axis=1)


def head_masks():
    head_of = lax.broadcasted_iota(jnp.int32, (1, GROUP), 1) // HEAD_DIM
    in_head = [head_of == h for h in range(PER_GROUP)]
    return in_head, [jnp.where(m, 1.0, 0.0).astype(BF16) for m in in_head]


def column(row):
    return jnp.broadcast_to(row, (8, row.shape[1])).T[:, 0:1]


def tile_product(tiles, right):
    rows = right.shape[0]
    res = [None] * (rows // BLOCK)
    for t, left in enumerate(tiles):
        part = mm(left, right[t * GROUP : (t + 1) * GROUP])
        first = tile_rows(t, rows)[0] // BLOCK
        for i in range(left.shape[0] // BLOCK):
            piece = part[i * BLOCK : (i + 1) * BLOCK]
            res[first + i] = piece if res[first + i] is None else res[first + i] + piece
    return jnp.concatenate(res, axis=0)


def stacked_scores(left, right, keep):
    rows = left.shape[0]
    found = []
    for t in range(rows // GROUP):
        lo, hi = tile_rows(t, rows)
        stack = jnp.concatenate([left[lo:hi] * keep[h] for h in range(PER_GROUP)], axis=0)
        found.append(mm(stack, right[t * GROUP : (t + 1) * GROUP], NT))
    return found


def attend_kernel(*refs, parts, unit, fresh):
    pieces = refs[:parts]
    seg_ref, gain_ref, shift_ref, bias_ref, down_ref, up_ref, pos_hbm, wqkv_hbm, wo_hbm = refs[
        parts : parts + 9
    ]
    refs = refs[parts + 9 + (0 if fresh else 6) :]
    outs, (x4, pos, wqkv, wo, start, xb, normed0, q, k, v, red, pr, probs, mixed, sems) = (
        refs[:6],
        refs[6:],
    )
    rows, width = normed0.shape
    groups = width // GROUP
    blocks = rows // BLOCK
    tiles = rows // GROUP
    row_parts = [slice(i, i + STEP_ROWS) for i in range(0, rows, STEP_ROWS)]
    me = lax.axis_index("tensor")

    in_copies = [
        pltpu.make_async_copy(piece, x4.at[jnp.bitwise_xor(me, r)], sems.at[r])
        for r, piece in enumerate(pieces)
    ]
    pos_copy = pltpu.make_async_copy(pos_hbm, pos, sems.at[parts])
    qkv_copy = pltpu.make_async_copy(wqkv_hbm, wqkv, sems.at[parts + 1])
    wo_copy = pltpu.make_async_copy(wo_hbm, wo, sems.at[parts + 2])
    start_out, k_out, v_out, red_out, pr_out = [
        pltpu.make_async_copy(ref, out.at[unit], sems.at[parts + 3 + i])
        for i, (ref, out) in enumerate(zip((start, k, v, red, pr), outs))
    ]

    def probs_copy(g):
        heads = pl.ds(g * PER_GROUP, PER_GROUP)
        return pltpu.make_async_copy(
            probs.at[heads], outs[5].at[unit, heads], sems.at[parts + 8 + g]
        )

    for copy in [pos_copy, *in_copies, qkv_copy, wo_copy]:
        copy.start()

    seg_row = seg_ref[unit].astype(F32)
    seg_col = column(seg_row)
    lane = lax.broadcasted_iota(jnp.int32, (rows, rows), 1)
    sub = lax.broadcasted_iota(jnp.int32, (rows, rows), 0)
    before = (seg_col == seg_row) & (lane < sub)
    place = jnp.sum(jnp.where(before, 1.0, 0.0), axis=1, keepdims=True).astype(jnp.int32)
    one_hot = jnp.where(lane == place, 1.0, 0.0).astype(BF16)
    pos_copy.wait()
    start[...] = mm(one_hot, pos[...])
    for copy in in_copies:
        copy.wait()
    start[...] += jnp.concatenate([x4[t] for t in range(parts)], axis=1).astype(F32)

    gain0, shift0 = gain_ref[0:1], shift_ref[0:1]
    for part in row_parts:
        x = start[part, :]
        off = x - row_mean(x)
        y = off * lax.rsqrt(row_mean(off * off) + LN_EPS) * gain0 + shift0
        normed0[part, :] = y + bias_ref[3:4]
        xb[part, :] = y.astype(BF16)

    rank = up_ref.shape[1]
    spot = lax.broadcasted_iota(jnp.int32, (rank, GROUP), 1) % HEAD_DIM
    line = lax.broadcasted_iota(jnp.int32, (rank, GROUP), 0)
    lows = [mm(xb[...], down_ref[i]).astype(BF16) for i in range(2)]
    ups = [up_ref[i].astype(BF16) * BF16(2.0) for i in range(2)]
    red[...] = add_all(
        [
            mm(low, jnp.where(spot == line + i * rank, 1.0, 0.0).astype(BF16))
            for i, low in enumerate(lows)
        ]
    ).astype(BF16)
    red_out.start()

    in_head, keep = head_masks()

    def far(b, c):
        hit = seg_col[b * BLOCK : (b + 1) * BLOCK] == seg_row[:, c * BLOCK : (c + 1) * BLOCK]
        return jnp.where(hit, 0.0, -1e9)

    away = {
        (b, c): far(b, c) for b in range(blocks) for c in range(max(b - 1, 0), min(b + 2, blocks))
    }
    memo = {}

    def project(g):
        lanes = slice(g * GROUP, (g + 1) * GROUP)

        def queries():
            new = mm(xb[...], wqkv[0, :, lanes]) + mm(lows[0], ups[0][:, lanes])
            q[:, lanes] = (new + bias_ref[0:1, lanes]).astype(BF16) * BF16(HEAD_DIM**-0.5)

        def keys():
            k[:, lanes] = (mm(xb[...], wqkv[1, :, lanes]) + bias_ref[1:2, lanes]).astype(BF16)

        def values():
            new = mm(xb[...], wqkv[2, :, lanes]) + mm(lows[1], ups[1][:, lanes])
            v[:, lanes] = (new + bias_ref[2:3, lanes]).astype(BF16)

        return [queries, keys, values]

    def attention(g):
        lanes = slice(g * GROUP, (g + 1) * GROUP)

        def begin():
            memo["scores"] = stacked_scores(q[:, lanes], k[:, lanes], keep)
            memo["out"] = jnp.zeros((rows, GROUP), F32)
            memo["low"] = jnp.zeros((rows, GROUP), F32)

        def one_head(h):
            vrh = v[:, lanes] * keep[h] + red[...] * (1 - keep[h])
            prob_tiles = [[] for _ in range(tiles)]
            for b in range(blocks):
                found = []
                for t, lo, hi in block_pieces(b, blocks):
                    first, last = tile_rows(t, rows)
                    top = h * (last - first) + b * BLOCK - first
                    lane_at = slice((lo - 2 * t) * BLOCK, (hi + 1 - 2 * t) * BLOCK)
                    s = memo["scores"][t][top : top + BLOCK, lane_at]
                    found.append(
                        s + jnp.concatenate([away[b, c] for c in range(lo, hi + 1)], axis=1)
                    )
                peak = functools.reduce(
                    jnp.maximum, [jnp.max(s, axis=1, keepdims=True) for s in found]
                )
                found = [jnp.exp(s - peak) for s in found]
                inv = 1.0 / add_all([jnp.sum(s, axis=1, keepdims=True) for s in found])
                for (t, lo, hi), s in zip(block_pieces(b, blocks), found):
                    prob_tiles[t].append(spread((s * inv).astype(BF16), t, lo, hi))
            prob_tiles = [jnp.concatenate(tile, axis=0) for tile in prob_tiles]
            for t, tile in enumerate(prob_tiles):
                probs[g * PER_GROUP + h, t, 0 : tile.shape[0], :] = tile
            res = tile_product(prob_tiles, vrh)
            memo["out"] = jnp.where(in_head[h], res, memo["out"])
            memo["low"] = jnp.where(in_head[(h + 1) % PER_GROUP], res, memo["low"])

        def end():
            mixed[:, lanes] = memo["out"].astype(BF16)
            pr[:, lanes] = memo["low"].astype(BF16)
            probs_copy(g).start()

        return [begin] + [functools.partial(one_head, h) for h in range(PER_GROUP)] + [end]

    def output(g):
        def step(n):
            lanes = slice(n, n + GROUP)
            add = mm(mixed[:, g * GROUP : (g + 1) * GROUP], wo[g * GROUP : (g + 1) * GROUP, lanes])
            start[:, lanes] = (normed0 if g == 0 else start)[:, lanes] + add

        return [functools.partial(step, n) for n in range(0, width, GROUP)]

    qkv_copy.wait()
    interleave(project(0))
    wo_copy.wait()
    for g in range(groups):
        others = project(g + 1) if g + 1 < groups else []
        if g + 1 == groups:
            k_out.start()
            v_out.start()
        interleave(attention(g), others + (output(g - 1) if g else []))
    pr_out.start()
    interleave(output(groups - 1))
    start_out.start()
    for copy in [start_out, k_out, v_out, red_out, pr_out] + [probs_copy(g) for g in range(groups)]:
        copy.wait()


def attend_call(pieces, seg, small, wqkv, wo, kept, unit, units):
    pos, gain, shift, bias, down, up = small
    parts = len(pieces)
    rows, feats = pieces[0].shape
    width = pos.shape[1]
    heads = width // HEAD_DIM
    tiles = rows // GROUP
    forms = [
        ((rows, width), F32),
        ((rows, width), BF16),
        ((rows, width), BF16),
        ((rows, GROUP), BF16),
        ((rows, width), BF16),
        ((heads, tiles, SPAN, GROUP), BF16),
    ]
    fresh = kept is None
    scratch = [
        pltpu.VMEM((parts, rows, feats), BF16),
        pltpu.VMEM(pos.shape, BF16),
        pltpu.VMEM(wqkv.shape, BF16),
        pltpu.VMEM(wo.shape, BF16),
        pltpu.VMEM((rows, width), F32),
        pltpu.VMEM((rows, width), BF16),
        pltpu.VMEM((rows, width), F32),
        pltpu.VMEM((rows, width), BF16),
        pltpu.VMEM((rows, width), BF16),
        pltpu.VMEM((rows, width), BF16),
        pltpu.VMEM((rows, GROUP), BF16),
        pltpu.VMEM((rows, width), BF16),
        pltpu.VMEM((heads, tiles, SPAN, GROUP), BF16),
        pltpu.VMEM((rows, width), BF16),
        pltpu.SemaphoreType.DMA((parts + 8 + width // GROUP,)),
    ]
    args = [*pieces, seg, gain, shift, bias, down, up, pos, wqkv, wo]
    aliases = {} if fresh else {len(args) + i: i for i in range(len(forms))}
    return pl.pallas_call(
        functools.partial(attend_kernel, parts=parts, unit=unit, fresh=fresh),
        out_shape=[jax.ShapeDtypeStruct((units, *shape), kind) for shape, kind in forms],
        in_specs=[ANY] * parts + [VMEM] * 6 + [ANY] * 3 + ([] if fresh else [ANY] * len(forms)),
        out_specs=[ANY] * len(forms),
        input_output_aliases=aliases,
        scratch_shapes=scratch,
        compiler_params=pltpu.CompilerParams(vmem_limit_bytes=58 * MIB),
        cost_estimate=pl.CostEstimate(
            flops=rows * width,
            bytes_accessed=MIB // 4,
            transcendentals=0,
        ),
        name="attend",
    )(*args, *([] if fresh else kept))


def finish_kernel(*refs, plan, arrays, parts):
    seg_ref, label_ref, gain_ref, shift_ref, bias_ref, head_ref, wo_hbm, *refs = refs
    weight_refs, refs = refs[:arrays], refs[arrays:]
    kept, refs = refs[:6], refs[6:]
    acc_ref, refs = refs[0], refs[1:]
    bufs, refs = (refs[:6], refs[6:12]), refs[12:]
    xbs, xh1s, stats, refs = refs[:3], refs[3:6], refs[6:9], refs[9:]
    accs, slopes, acts, refs = refs[:2], refs[2:4], refs[4:6], refs[6:]
    wo, win, wout, ffb, mixed, sems, wsems = refs
    units = kept[0].shape[0]
    rows, width = mixed.shape
    hidden_part = win.shape[2]
    chunk = GROUP if hidden_part % GROUP == 0 else hidden_part
    groups = width // GROUP
    blocks = rows // BLOCK
    tiles = rows // GROUP
    row_parts = [slice(i, i + STEP_ROWS) for i in range(0, rows, STEP_ROWS)]
    chunks = [(r, c) for r in range(parts) for c in range(0, hidden_part, chunk)]
    half = lax.rem(lax.axis_index("dp"), 2)

    weight_copies = [[], [], [], []]
    for i, (matrix, array, first, n, r, mine) in enumerate(plan):
        dst = (win, wout, ffb)[matrix].at[r]
        if mine is not None:
            top = pl.multiple_of((half if mine else 1 - half) * n, 16)
            dst = (win, wout, ffb)[matrix].at[r, pl.ds(top, n), :]
        src = weight_refs[array].at[pl.ds(first, n), :]
        weight_copies[matrix].append(pltpu.make_async_copy(src, dst, wsems.at[i]))
    weight_copies[3].append(pltpu.make_async_copy(wo_hbm, wo, wsems.at[len(plan)]))

    state_copies = [
        [
            pltpu.make_async_copy(src.at[u], buf, sems.at[u % 2, i])
            for i, (src, buf) in enumerate(zip(kept, bufs[u % 2]))
        ]
        for u in range(units)
    ]

    def start(copies):
        for copy in copies:
            copy.start()

    def wait(copies):
        for copy in copies:
            copy.wait()

    start(state_copies[0][:1] + weight_copies[2] + weight_copies[0] + weight_copies[1])
    for u in range(1, min(2, units)):
        start(state_copies[u][:1])
    start(weight_copies[3] + state_copies[0][1:])

    gain1, gain2 = gain_ref[1:2], gain_ref[2:3]
    shift1, shift2 = shift_ref[1:2], shift_ref[2:3]
    head_row = head_ref[...].reshape(1, width + 1)
    head, head_bias = head_row[:, 0:width], head_row[:, width : width + 1]
    hg = head * gain2
    hg_mean = row_mean(hg)
    bias4 = bias_ref[4:5]
    base = jnp.sum(shift2 * head, axis=1, keepdims=True)
    in_head, keep = head_masks()
    acc_ref[...] = jnp.zeros(acc_ref.shape, F32)

    def norm1(u):
        resid, xb, xh1, stat1 = bufs[u % 2][0], xbs[u % 3], xh1s[u % 3], stats[u % 3]

        def step(part):
            x = resid[part, :]
            off = x - row_mean(x)
            inv = lax.rsqrt(row_mean(off * off) + LN_EPS)
            xh = off * inv
            xh1[part, :] = xh
            stat1[part, :] = inv
            xb[part, :] = (xh * gain1 + shift1).astype(BF16)

        return [lambda: wait(state_copies[u][:1])] + [
            functools.partial(step, part) for part in row_parts
        ]

    def hidden(r, c):
        return slice(r * hidden_part + c, r * hidden_part + c + chunk)

    def feed_in(u):
        xb, act, slope = xbs[u % 3], acts[u % 2], slopes[u % 2]

        def step(r, c):
            line = ffb[r, 0:1, c : c + chunk].astype(F32)
            pre = mm(xb[...], win[r, :, c : c + chunk]) + line
            phi = 0.5 + 0.5 * lax.erf(pre * INV_SQRT2)
            act[:, hidden(r, c)] = (pre * phi).astype(BF16)
            tail = pre * jnp.exp(-0.5 * pre * pre) * INV_SQRT_2PI
            slope[:, hidden(r, c)] = (phi + tail).astype(BF16)

        return [functools.partial(step, r, c) for r, c in chunks]

    def feed_out(u):
        act, acc = acts[u % 2], accs[u % 2]

        def step(n, r):
            lanes = slice(n, n + GROUP)
            add = mm(act[:, r * hidden_part : (r + 1) * hidden_part], wout[r, :, lanes])
            acc[:, lanes] = add if r == 0 else acc[:, lanes] + add

        return [
            functools.partial(step, n, r) for n in range(0, width, GROUP) for r in range(parts)
        ]

    def head_part(u):
        xb, xh1, acc = xbs[u % 3], xh1s[u % 3], accs[u % 2]
        memo = {"inv": [], "dots": [], "grad": jnp.zeros((8, width), F32)}

        def norm2(part):
            x = xh1[part, :] * gain1 + shift1 + (acc[part, :] + bias4)
            off = x - row_mean(x)
            inv = lax.rsqrt(row_mean(off * off) + LN_EPS)
            xh = off * inv
            acc[part, :] = xh
            memo["inv"].append(inv)
            memo["dots"].append(jnp.sum(xh * hg, axis=1, keepdims=True))

        def items():
            dots = jnp.concatenate(memo["dots"], axis=0)
            seg_row = seg_ref[u].astype(F32)
            seg_col = column(seg_row)
            label = label_ref[u]
            slots = label.shape[1]
            slot_no = lax.broadcasted_iota(jnp.int32, (rows, slots), 1).astype(F32)
            member = jnp.where(seg_col == slot_no, 1.0, 0.0)
            counts = jnp.sum(member, axis=0, keepdims=True)
            sums = jnp.sum(member * (dots + base), axis=0, keepdims=True)
            most = jnp.maximum(counts, 1.0)
            error = jnp.where(counts > 0, sums / most + head_bias - label, 0.0)
            grad_pred = 2.0 * error
            memo["weight"] = jnp.sum(member * (grad_pred / most), axis=1, keepdims=True)
            loss = jnp.sum(error * error, axis=1, keepdims=True)
            weight_sum = jnp.sum(grad_pred, axis=1, keepdims=True)
            memo["sum"] = weight_sum
            count = jnp.max(seg_row, axis=1, keepdims=True) + 1.0
            lane_row = lax.broadcasted_iota(jnp.int32, (1, width), 1)
            acc_ref[17:18, :] += jnp.where(
                lane_row == 0,
                loss,
                jnp.where(lane_row == 1, count, jnp.where(lane_row == 2, weight_sum, 0.0)),
            )

        def back2(i, part):
            xh = acc[part, :]
            w = memo["weight"][part]
            weighted = xh * w
            for j in range(STEP_ROWS // 8):
                memo["grad"] = memo["grad"] + weighted[j * 8 : (j + 1) * 8]
            scaled = memo["dots"][i] * (1.0 / width)
            grad = (memo["inv"][i] * w) * (hg - hg_mean - xh * scaled)
            acc[part, :] = grad
            xb[part, :] = grad.astype(BF16)

        def close():
            total = jnp.sum(memo["grad"], axis=0, keepdims=True)
            acc_ref[16:17, :] += total * gain2 + memo["sum"] * shift2

        return (
            [functools.partial(norm2, part) for part in row_parts]
            + [items]
            + [functools.partial(back2, i, part) for i, part in enumerate(row_parts)]
            + [close]
        )

    def feed_back(u):
        xb, act, slope, acc = xbs[u % 3], acts[u % 2], slopes[u % 2], accs[u % 2]

        def up(r, c):
            back = mm(xb[...], wout[r, c : c + chunk, :], NT)
            act[:, hidden(r, c)] = (back * slope[:, hidden(r, c)].astype(F32)).astype(BF16)

        def down(n, r):
            lanes = slice(n, n + GROUP)
            acc[:, lanes] += mm(
                act[:, r * hidden_part : (r + 1) * hidden_part], win[r, lanes, :], NT
            )

        return [functools.partial(up, r, c) for r, c in chunks] + [
            functools.partial(down, n, r) for n in range(0, width, GROUP) for r in range(parts)
        ]

    def attention_back(u):
        xb, xh1, stat1, acc = xbs[u % 3], xh1s[u % 3], stats[u % 3], accs[u % 2]
        _, k2, v2, red2, pr2, probs2 = bufs[u % 2]
        memo = {}

        def back1(part):
            g = acc[part, :] * gain1
            xh = xh1[part, :]
            grad = stat1[part, :] * (g - row_mean(g) - xh * row_mean(g * xh))
            xb[part, :] = grad.astype(BF16)

        def project(n):
            mixed[:, n : n + GROUP] = mm(xb[...], wo[n : n + GROUP, :], NT).astype(BF16)

        def begin(g):
            lanes = slice(g * GROUP, (g + 1) * GROUP)
            memo["grads"] = stacked_scores(mixed[:, lanes], v2[:, lanes], keep)
            memo["out"] = jnp.zeros((rows, GROUP), F32)

        def one_head(g, h):
            lanes = slice(g * GROUP, (g + 1) * GROUP)
            score_tiles = [[] for _ in range(tiles)]
            for b in range(blocks):
                found = []
                for t, lo, hi in block_pieces(b, blocks):
                    first, last = tile_rows(t, rows)
                    top = b * BLOCK - first
                    lane_at = slice((lo - 2 * t) * BLOCK, (hi + 1 - 2 * t) * BLOCK)
                    here = h * (last - first) + top
                    dp = memo["grads"][t][here : here + BLOCK, lane_at]
                    p = probs2[g * PER_GROUP + h, t, top : top + BLOCK, lane_at]
                    found.append((p.astype(F32), dp))
                shared = add_all([jnp.sum(p * dp, axis=1, keepdims=True) for p, dp in found])
                for (t, lo, hi), (p, dp) in zip(block_pieces(b, blocks), found):
                    score_tiles[t].append(spread((p * (dp - shared)).astype(BF16), t, lo, hi))
            tiles_ = [jnp.concatenate(tile, axis=0) for tile in score_tiles]
            memo["out"] = jnp.where(in_head[h], tile_product(tiles_, k2[:, lanes]), memo["out"])

        def end(g):
            lanes = slice(g * GROUP, (g + 1) * GROUP)
            query_part = mm(red2[...], memo["out"].astype(BF16), TN)[0:8]
            acc_ref[0:8, lanes] += query_part * (2.0 * HEAD_DIM**-0.5)
            cross = mm(pr2[:, lanes], mixed[:, lanes], TN)
            value_part = jnp.zeros((8, GROUP), F32)
            for h in range(PER_GROUP):
                top = ((h + 1) % PER_GROUP) * HEAD_DIM + 8
                value_part = jnp.where(in_head[h], cross[top : top + 8], value_part)
            acc_ref[8:16, lanes] += 2.0 * value_part

        steps = [functools.partial(back1, part) for part in row_parts]
        if u == 0:
            steps.append(lambda: wait(weight_copies[3]))
        steps += [functools.partial(project, n) for n in range(0, width, GROUP)]
        steps.append(lambda: wait(state_copies[u][1:]))
        for g in range(groups):
            steps.append(functools.partial(begin, g))
            steps += [functools.partial(one_head, g, h) for h in range(PER_GROUP)]
            steps.append(functools.partial(end, g))
        return steps

    interleave(norm1(0))
    wait(weight_copies[2] + weight_copies[0])
    interleave(feed_in(0))
    wait(weight_copies[1])
    interleave(feed_out(0), norm1(1) if units > 1 else [])
    for u in range(units):
        later = u + 1 < units
        if u + 2 < units:
            start(state_copies[u + 2][:1])
        if later:
            start(state_copies[u + 1][1:])
        interleave(head_part(u), feed_in(u + 1) if later else [])
        interleave(feed_back(u), norm1(u + 2) if u + 2 < units else [])
        interleave(attention_back(u), feed_out(u + 1) if later else [])


def finish_call(segs, labels, small, wo, arrays, plan, kept, parts):
    gain, shift, bias, head = small
    units, rows, width = kept[0].shape
    hidden_part = arrays[0].shape[1]
    hidden = hidden_part * parts
    scratch = [pltpu.VMEM(a.shape[1:], a.dtype) for a in kept] * 2
    scratch += [pltpu.VMEM((rows, width), BF16)] * 3
    scratch += [pltpu.VMEM((rows, width), F32)] * 3
    scratch += [pltpu.VMEM((rows, 1), F32)] * 3
    scratch += [pltpu.VMEM((rows, width), F32)] * 2
    scratch += [pltpu.VMEM((rows, hidden), BF16)] * 4
    scratch += [
        pltpu.VMEM(wo.shape, BF16),
        pltpu.VMEM((parts, width, hidden_part), BF16),
        pltpu.VMEM((parts, hidden_part, width), BF16),
        pltpu.VMEM((parts, BIAS_ROWS, hidden_part), BF16),
        pltpu.VMEM((rows, width), BF16),
        pltpu.SemaphoreType.DMA((2, len(kept))),
        pltpu.SemaphoreType.DMA((len(plan) + 1,)),
    ]
    return pl.pallas_call(
        functools.partial(finish_kernel, plan=plan, arrays=len(arrays), parts=parts),
        out_shape=jax.ShapeDtypeStruct((ACC_ROWS, width), F32),
        in_specs=[VMEM] * 6 + [ANY] * (1 + len(arrays) + len(kept)),
        out_specs=VMEM,
        scratch_shapes=scratch,
        compiler_params=pltpu.CompilerParams(vmem_limit_bytes=62 * MIB),
        name="finish",
    )(segs, labels, gain, shift, bias, head, wo, *arrays, *kept)


def update_kernel(
    acc_ref,
    other_ref,
    up_ref,
    momentum_ref,
    head_ref,
    first_ref,
    second_ref,
    loss_ref,
    items_ref,
    norm_ref,
    moment_out,
    up_out,
    low_out,
    first_out,
    second_out,
    head_out,
    head_low_out,
):
    total = acc_ref[...] + other_ref[...]
    width = total.shape[1]
    rank = up_ref.shape[0] // 2
    items = total[17:18, 1:2]
    loss_ref[...] = total[17:18, 0:1]
    items_ref[...] = items
    adapter = total[0:16] / items
    head_grad = jnp.concatenate([total[16:17], total[17:18, 2:3]], axis=1) / items
    norm = jnp.sqrt(jnp.sum(adapter * adapter) + jnp.sum(head_grad * head_grad))
    norm_ref[...] = jnp.full((1, 1), norm, F32)
    factor = jnp.minimum(1.0, CLIP_NORM / (norm_ref[...] + 1e-06))
    moment = ORTHO_MOMENTUM * momentum_ref[...] + factor * adapter
    moment_out[...] = moment

    def dot(left, right, dims=NN):
        return lax.dot_general(
            left, right, dims, preferred_element_type=F32, precision=lax.Precision.HIGHEST
        )

    basis = []
    for i in range(2):
        part = moment[i * rank : (i + 1) * rank]
        size = jnp.sqrt(jnp.sum(jnp.sum(part * part, axis=1, keepdims=True), axis=0, keepdims=True))
        basis.append(part / (size + 1e-07))
    for sweep in range(5):
        gram = [dot(x, x, NT) for x in basis]
        poly = [NS_B * g + NS_C * dot(g, g) for g in gram]
        basis = [NS_A * x + dot(p, x) for x, p in zip(basis, poly)]
    up = up_ref[...] - ORTHO_STEP_SIZE * jnp.concatenate(basis, axis=0)
    up_out[...] = up
    low_out[...] = up.astype(BF16)

    clipped = factor * head_grad
    def as_row(ref):
        return ref[...].reshape(1, width + 1)

    first = BETA_ONE * as_row(first_ref) + (1.0 - BETA_ONE) * clipped
    second = BETA_TWO * as_row(second_ref) + (1.0 - BETA_TWO) * clipped * clipped
    first_hat = first / (1.0 - BETA_ONE**STEP)
    second_hat = second / (1.0 - BETA_TWO**STEP)
    head = as_row(head_ref)
    new_head = head - ADAM_RATE * (first_hat / (jnp.sqrt(second_hat) + ADAM_EPS) + DECAY * head)
    first_out[...] = first[0]
    second_out[...] = second[0]
    head_out[...] = new_head[0]
    head_low_out[...] = new_head[0].astype(BF16)


def update_call(acc, other, up, momentum, head, first, second):
    one = jax.ShapeDtypeStruct((1, 1), F32)
    flat = jax.ShapeDtypeStruct(up.shape, F32)
    row = jax.ShapeDtypeStruct(head.shape, F32)
    return pl.pallas_call(
        update_kernel,
        out_shape=[
            one,
            one,
            one,
            flat,
            flat,
            jax.ShapeDtypeStruct(up.shape, BF16),
            row,
            row,
            row,
            jax.ShapeDtypeStruct(head.shape, BF16),
        ],
        in_specs=[VMEM] * 7,
        out_specs=[VMEM] * 10,
        name="update",
    )(acc, other, up, momentum, head, first, second)


def swap(value, axis, bit):
    size = lax.axis_size(axis)
    return lax.ppermute(value, axis, [(i, i ^ bit) for i in range(size)])


class Weights:
    def __init__(self, owns, bias, after):
        parts = lax.axis_size("tensor")
        half = lax.rem(lax.axis_index("dp"), 2)
        self.owns = owns
        self.sizes = [own.shape[0] // 2 for own in owns]
        self.bias = jnp.pad(bias[None, :], ((0, BIAS_ROWS - 1), (0, 0)))
        cuts = [
            lax.dynamic_slice_in_dim(own, half * n, n, 0) for own, n in zip(owns, self.sizes)
        ]
        if cuts[0].shape[1] == cuts[1].shape[1]:
            cuts = [jnp.concatenate([*cuts, self.bias], axis=0)]
        else:
            cuts.append(self.bias)
        self.one = len(cuts) == 1
        cuts, self.first = lax.optimization_barrier((cuts, after))
        mine = {0: cuts}
        bit = parts // 2
        while bit > 1:
            mine.update({r ^ bit: [swap(a, "tensor", bit) for a in mine[r]] for r in list(mine)})
            bit //= 2
        del mine[0]
        self.mine = mine

    def core(self, pieces):
        return {r ^ 1: [swap(a, "tensor", 1) for a in arrays] for r, arrays in pieces.items()}

    def across(self, pieces):
        return {r: [swap(a, "dp", 1) for a in arrays] for r, arrays in pieces.items()}

    def operands(self):
        arrays = [*self.owns, *self.core_own, self.bias, self.core_bias]
        plan = [(2, 4, 0, BIAS_ROWS, 0, None), (2, 5, 0, BIAS_ROWS, 1, None)]
        for i in range(2):
            n = 2 * self.sizes[i]
            plan += [(i, i, 0, n, 0, None), (i, 2 + i, 0, n, 1, None)]
        for pieces, is_mine in (
            (self.mine, True),
            (self.core_mine, True),
            (self.other, False),
            (self.core_other, False),
        ):
            for r, found in pieces.items():
                first = 0
                for i, n in enumerate([*self.sizes, BIAS_ROWS]):
                    array = len(arrays) + (0 if self.one else i)
                    if i < 2:
                        plan.append((i, array, first, n, r, is_mine))
                    elif is_mine:
                        plan.append((i, array, first, n, r, None))
                    first += n if self.one else 0
                arrays += found
        return arrays, tuple(sorted(plan, key=lambda step: step[0]))


def local(
    input_token_ids,
    segments,
    labels,
    embedding,
    position_embedding_table,
    norm_gain_rows,
    norm_shift_rows,
    query_key_value_weight,
    attention_output_weight,
    attention_bias_stack,
    feedforward_in_weight,
    feedforward_bias,
    feedforward_out_weight,
    adapter_down_weight,
    adapter_up_weight,
    adapter_momentum,
    head,
    head_first_moment,
    head_second_moment,
):
    length = input_token_ids.shape[-1]
    slots = labels.shape[-1]
    width = position_embedding_table.shape[1]
    rank = adapter_up_weight.shape[1]
    parts = lax.axis_size("tensor")
    ids = input_token_ids.reshape(-1, 1, length)
    all_ids = [ids] + [swap(ids, "tensor", r) for r in range(1, parts)]
    segs = segments.reshape(-1, 1, length)
    labs = labels.reshape(-1, 1, slots)
    units = ids.shape[0]


    weights = Weights([feedforward_in_weight, feedforward_out_weight], feedforward_bias, all_ids)
    all_ids, owns = lax.optimization_barrier((weights.first, weights.owns))
    weights.core_own = [swap(own, "tensor", 1) for own in owns]
    weights.core_bias = swap(weights.bias, "tensor", 1)
    picked = embed_call(all_ids, embedding)
    (
        picked,
        weights.mine,
        weights.core_own,
        weights.core_bias,
        head_rows,
    ) = lax.optimization_barrier(
        (
            picked,
            weights.mine,
            weights.core_own,
            weights.core_bias,
            (head, head_first_moment, head_second_moment),
        )
    )
    picked = [picked[u * parts : (u + 1) * parts] for u in range(units)]

    small = (
        position_embedding_table,
        norm_gain_rows,
        norm_shift_rows,
        attention_bias_stack,
        adapter_down_weight,
        adapter_up_weight,
    )
    kept = None
    moved = []
    for u in range(units):
        while len(moved) < min(u + 2, units):
            sends = picked[len(moved)][1:]
            if moved:
                sends = lax.optimization_barrier((sends, moved[-1], kept))[0]
            moved.append([swap(a, "tensor", r + 1) for r, a in enumerate(sends)])
        if u == units - 1:
            other, moved[u], _ = lax.optimization_barrier((weights.other, moved[u], kept))
            weights.core_other = weights.core(other)
        if u == 0:
            mine, moved[0] = lax.optimization_barrier((weights.mine, moved[0]))
            weights.other = weights.across(mine)
            weights.core_mine = weights.core(mine)
        kept = attend_call(
            [picked[u][0], *moved[u]],
            segs,
            small,
            query_key_value_weight,
            attention_output_weight,
            kept,
            u,
            units,
        )

    arrays, plan = weights.operands()
    acc = finish_call(
        segs,
        labs,
        (norm_gain_rows, norm_shift_rows, attention_bias_stack, head_rows[0]),
        attention_output_weight,
        arrays,
        plan,
        kept,
        parts,
    )
    steps = []
    for axis in ("tensor", "dp"):
        bit = 1
        while bit < lax.axis_size(axis):
            steps.append((axis, bit))
            bit *= 2
    for axis, bit in steps[:-1]:
        acc = acc + swap(acc, axis, bit)
    other = swap(acc, *steps[-1])

    flat = (2 * rank, width)
    outs = update_call(
        acc,
        other,
        adapter_up_weight.reshape(flat),
        adapter_momentum.reshape(flat),
        *head_rows,
    )
    loss, items, norm, moment, new_up, low, first, second, new_head, head_low = outs
    shape = adapter_up_weight.shape
    return (
        loss[0, 0],
        items[0, 0],
        norm[0, 0],
        moment.reshape(shape),
        new_up.reshape(shape),
        low.reshape(shape),
        first,
        second,
        new_head,
        head_low,
    )


def solution(mesh):
    rows = P(None, ("dp", "tensor"), None)
    placed = (
        (rows, rows, rows, P("tensor", None))
        + (P(),) * 6
        + (P(None, "tensor"), P("tensor"), P("tensor", None))
        + (P(),) * 6
    )
    return jax.shard_map(
        local, mesh=mesh, in_specs=placed, out_specs=(P(),) * 10, check_vma=False
    )
```

profile of v0, /device:TPU:0, one launch (start us, length us, event | category | flops | bytes accessed | tf_op | source)
XLA Modules:
  0.0 220.0 jit_solution(18281611055977710053)
XLA Ops:
  1.2 2.6 %collective-permute-start.1 = (s32[4,1,512]{2,1,0:T(1,128)}, s32[4,1,512]{2,1,0:T(1,128)S(1)}, u32[]{:S(2)}, u32[]{:S(2)}) collective-permute-start(s32[4,1,512]{2,1,0:T(1,128)} %refs_0_.1), channel_id=1, source_target_pairs={{0,2},{1,3},{2,0},{3,1},{4,6},{5,7},{6,4},{7,5},{8,10},{9,11},{10,... | collective-permute-start | bytes 24584 | tf_op jit(solution)/shard_map/ppermute | solution.py:823
  4.5 1.3 constant_dynamic-slice_fusion
  5.8 1.2 pad_maximum_fusion
  7.1 1.8 collective-permute-start.3
  9.4 29.7 %embed.1 = (bf16[512,192]{1,0:T(8,128)(2,1)}, bf16[512,192]{1,0:T(8,128)(2,1)}, bf16[512,192]{1,0:T(8,128)(2,1)}, bf16[512,192]{1,0:T(8,128)(2,1)}, bf16[512,192...) custom-call(s32[4,1,512]{2,1,0:T(1,128)} %refs_0_.1, ...), custom_call_target="tpu_custom_call" | custom-call | tf_op jit(solution)/shard_map/embed/pallas_call | solution.py:147
  40.0 1.1 collective-permute-start.9
  41.2 7.9 %collective-permute-done.8.refs_2_ = bf16[512,192]{1,0:T(8,128)(2,1)S(1)} collective-permute-done((bf16[512,192]{1,0:T(8,128)(2,1)}, bf16[512,192]{1,0:T(8,128)(2,1)S(1)}, u32[]{:S(2)}, u32[]{:S(2)}) %collective-permute-start.8) | collective-permute-done | bytes 196640 | tf_op jit(solution)/shard_map/ppermute | solution.py:823
  49.1 3.9 %collective-permute-done.9.refs_3_ = bf16[512,192]{1,0:T(8,128)(2,1)S(1)} collective-permute-done((bf16[512,192]{1,0:T(8,128)(2,1)}, bf16[512,192]{1,0:T(8,128)(2,1)S(1)}, u32[]{:S(2)}, u32[]{:S(2)}) %collective-permute-start.9) | collective-permute-done | bytes 196640 | tf_op jit(solution)/shard_map/ppermute | solution.py:823
  53.0 1.5 collective-permute-start.11
  55.4 0.9 collective-permute-start.14
  56.4 0.9 copy.47.refs_8_
  57.3 13.1 %attend.4 = (f32[4,512,768]{2,1,0:T(8,128)}, bf16[4,512,768]{2,1,0:T(8,128)(2,1)}, bf16[4,512,768]{2,1,0:T(8,128)(2,1)}, bf16[4,512,256]{2,1,0:T(8,128)(2,1)}, b...) custom-call(bf16[512,192]{1,0:T(8,128)(2,1)} %get-tuple-element.159.refs_0_, ...), custom_call_target="tpu_custom_call" | custom-call | flops 393216 | bytes 262144 | tf_op jit(solution)/shard_map/attend/pallas_call | solution.py:423
  70.6 0.8 collective-permute-start.15
  71.9 0.9 collective-permute-start.17
  72.8 13.4 %attend.5 = (f32[4,512,768]{2,1,0:T(8,128)}, bf16[4,512,768]{2,1,0:T(8,128)(2,1)}, bf16[4,512,768]{2,1,0:T(8,128)(2,1)}, bf16[4,512,256]{2,1,0:T(8,128)(2,1)}, b...) custom-call(bf16[512,192]{1,0:T(8,128)(2,1)} %get-tuple-element.172., ...), custom_call_target="tpu_custom_call", output_to_operand_aliasing={{0}: (13, {}), {1}: (14, {}), {2}: (15, {}), {3}: (16, {}),... | custom-call | flops 393216 | bytes 262144 | tf_op jit(solution)/shard_map/attend/pallas_call | solution.py:423
  86.3 0.8 collective-permute-start.18
  87.6 0.9 collective-permute-start.20
  88.5 0.7 collective-permute-start.10
  89.2 13.3 %attend.6 = (f32[4,512,768]{2,1,0:T(8,128)}, bf16[4,512,768]{2,1,0:T(8,128)(2,1)}, bf16[4,512,768]{2,1,0:T(8,128)(2,1)}, bf16[4,512,256]{2,1,0:T(8,128)(2,1)}, b...) custom-call(bf16[512,192]{1,0:T(8,128)(2,1)} %get-tuple-element.182., ...), custom_call_target="tpu_custom_call", output_to_operand_aliasing={{0}: (13, {}), {1}: (14, {}), {2}: (15, {}), {3}: (16, {}),... | custom-call | flops 393216 | bytes 262144 | tf_op jit(solution)/shard_map/attend/pallas_call | solution.py:423
  103.4 13.1 %attend.7 = (f32[4,512,768]{2,1,0:T(8,128)}, bf16[4,512,768]{2,1,0:T(8,128)(2,1)}, bf16[4,512,768]{2,1,0:T(8,128)(2,1)}, bf16[4,512,256]{2,1,0:T(8,128)(2,1)}, b...) custom-call(bf16[512,192]{1,0:T(8,128)(2,1)} %get-tuple-element.190., ...), custom_call_target="tpu_custom_call", output_to_operand_aliasing={{0}: (13, {}), {1}: (14, {}), {2}: (15, {}), {3}: (16, {}),... | custom-call | flops 393216 | bytes 262144 | tf_op jit(solution)/shard_map/attend/pallas_call | solution.py:423
  116.6 1.0 copy-done.2
  117.6 1.0 copy-done.3
  118.7 73.6 %finish.1 = f32[24,768]{1,0:T(8,128)} custom-call(s32[4,1,512]{2,1,0:T(1,128)} %refs_0_.2, f32[4,1,64]{2,1,0:T(1,128)} %refs_1_.1, f32[3,768]{1,0:T(4,128)} %refs_2_.1, f32[3,768]{1,0:T(4,128)} %refs_3_.1, f32[5,768]{1,0:T(8,128)} %refs_4_.11, f32[769]{0:T(1024)} %head_ref, bf16[768,768]{1,0:T(8,128)(2,1)} %refs_6_.9, bf16[768,768]{1,0:T(8,128)(2,1)} %refs_7_.9, ...), custom_call_target="tpu_custom_call" | custom-call | tf_op jit(solution)/shard_map/finish/pallas_call | solution.py:719
  192.4 1.5 collective-permute-done.22
  193.8 0.9 add.19
  195.3 3.8 %collective-permute-done.23 = f32[24,768]{1,0:T(8,128)S(1)} collective-permute-done((f32[24,768]{1,0:T(8,128)S(1)}, f32[24,768]{1,0:T(8,128)S(1)}, u32[]{:S(2)}, u32[]{:S(2)}) %collective-permute-start.23) | collective-permute-done | bytes 73760 | tf_op jit(solution)/shard_map/ppermute | solution.py:823
  199.7 3.8 %collective-permute-done.24 = f32[24,768]{1,0:T(8,128)S(1)} collective-permute-done((f32[24,768]{1,0:T(8,128)S(1)}, f32[24,768]{1,0:T(8,128)S(1)}, u32[]{:S(2)}, u32[]{:S(2)}) %collective-permute-start.24) | collective-permute-done | bytes 73760 | tf_op jit(solution)/shard_map/ppermute | solution.py:823
  203.6 1.6 collective-permute-start.25
  205.2 2.8 %collective-permute-done.25 = f32[24,768]{1,0:T(8,128)S(1)} collective-permute-done((f32[24,768]{1,0:T(8,128)S(1)}, f32[24,768]{1,0:T(8,128)S(1)}, u32[]{:S(2)}, u32[]{:S(2)}) %collective-permute-start.25) | collective-permute-done | bytes 73760 | tf_op jit(solution)/shard_map/ppermute | solution.py:823
  208.0 3.4 %collective-permute-start.26 = (f32[24,768]{1,0:T(8,128)S(1)}, f32[24,768]{1,0:T(8,128)S(1)}, u32[]{:S(2)}, u32[]{:S(2)}) collective-permute-start(f32[24,768]{1,0:T(8,128)S(1)} %add.22.acc_ref), channel_id=1, source_target_pairs={{0,16},{4,20},{8,24},{12,28},{16,0},{20,4},{24,8},{28,12},{1,17},{... | collective-permute-start | bytes 221192 | tf_op jit(solution)/shard_map/ppermute | solution.py:823
  211.4 3.1 %collective-permute-done.26.other_ref = f32[24,768]{1,0:T(8,128)S(1)} collective-permute-done((f32[24,768]{1,0:T(8,128)S(1)}, f32[24,768]{1,0:T(8,128)S(1)}, u32[]{:S(2)}, u32[]{:S(2)}) %collective-permute-start.26) | collective-permute-done | bytes 73760 | tf_op jit(solution)/shard_map/ppermute | solution.py:823
  215.2 4.7 %update.1 = (f32[1,1]{1,0:T(1,128)}, f32[1,1]{1,0:T(1,128)}, f32[1,1]{1,0:T(1,128)}, f32[16,768]{1,0:T(8,128)}, f32[16,768]{1,0:T(8,128)}, /*index=5*/bf16[16,76...) custom-call(f32[24,768]{1,0:T(8,128)} %copy-done.4, f32[24,768]{1,0:T(8,128)} %copy-done.18, ...), custom_call_target="tpu_custom_call" | custom-call | tf_op jit(solution)/shard_map/update/pallas_call | solution.py:801
  (98 shorter events, 7.6 us)
Async XLA Ops:
  0.7 6.4 %collective-permute-start = (s32[4,1,512]{2,1,0:T(1,128)}, s32[4,1,512]{2,1,0:T(1,128)S(1)}, u32[]{:S(2)}, u32[]{:S(2)}) collective-permute-start(s32[4,1,512]{2,1,0:T(1,128)} %refs_0_.1), channel_id=1, source_target_pairs={{0,1},{1,0},{2,3},{3,2},{4,5},{5,4},{6,7},{7,6},{8,9},{9,8},{10,11... | collective-permute-start | bytes 24584 | tf_op jit(solution)/shard_map/ppermute | solution.py:823
  1.2 5.8 %collective-permute-start.1 = (s32[4,1,512]{2,1,0:T(1,128)}, s32[4,1,512]{2,1,0:T(1,128)S(1)}, u32[]{:S(2)}, u32[]{:S(2)}) collective-permute-start(s32[4,1,512]{2,1,0:T(1,128)} %refs_0_.1), channel_id=1, source_target_pairs={{0,2},{1,3},{2,0},{3,1},{4,6},{5,7},{6,4},{7,5},{8,10},{9,11},{10,... | collective-permute-start | bytes 24584 | tf_op jit(solution)/shard_map/ppermute | solution.py:823
  3.7 3.3 %collective-permute-start.2 = (s32[4,1,512]{2,1,0:T(1,128)}, s32[4,1,512]{2,1,0:T(1,128)S(1)}, u32[]{:S(2)}, u32[]{:S(2)}) collective-permute-start(s32[4,1,512]{2,1,0:T(1,128)} %refs_0_.1), channel_id=1, source_target_pairs={{0,3},{1,2},{2,1},{3,0},{4,7},{5,6},{6,5},{7,4},{8,11},{9,10},{10,... | collective-permute-start | bytes 24584 | tf_op jit(solution)/shard_map/ppermute | solution.py:823
  4.5 34.7 %copy-start.17 = (bf16[16,768]{1,0:T(8,128)(2,1)}, bf16[16,768]{1,0:T(8,128)(2,1)S(1)}, u32[]{:S(2)}) copy-start(bf16[16,768]{1,0:T(8,128)(2,1)S(1)} %pad.4.refs_11_) | copy-start | bytes 73732
  7.0 49.3 %copy-start.20 = (bf16[2,768,8]{1,2,0:T(8,128)(2,1)S(1)}, bf16[2,768,8]{1,2,0:T(8,128)(2,1)}, u32[]{:S(2)}) copy-start(bf16[2,768,8]{1,2,0:T(8,128)(2,1)} %param.32) | copy-start | bytes 73732
  7.1 32.2 %collective-permute-start.3 = (bf16[784,768]{1,0:T(8,128)(2,1)}, bf16[784,768]{1,0:T(8,128)(2,1)}, u32[]{:S(2)}, u32[]{:S(2)}) collective-permute-start(bf16[784,768]{1,0:T(8,128)(2,1)} %pad_maximum_fusion), channel_id=1, source_target_pairs={{0,2},{1,3},{2,0},{3,1},{4,6},{5,7},{6,4},{7,5},{8,10},{9,11},{10,... | collective-permute-start | bytes 3612680 | tf_op jit(solution)/shard_map/ppermute | solution.py:823
  8.8 30.3 %collective-permute-start.4 = (bf16[768,768]{1,0:T(8,128)(2,1)S(1)}, bf16[768,768]{1,0:T(8,128)(2,1)}, u32[]{:S(2)}, u32[]{:S(2)}) collective-permute-start(bf16[768,768]{1,0:T(8,128)(2,1)S(1)} %copy-done), channel_id=1, source_target_pairs={{0,1},{1,0},{2,3},{3,2},{4,5},{5,4},{6,7},{7,6},{8,9},{9,8},{10,11... | collective-permute-start | bytes 3538952 | tf_op jit(solution)/shard_map/ppermute | solution.py:823
  8.9 30.3 %collective-permute-start.5 = (bf16[768,768]{1,0:T(8,128)(2,1)}, bf16[768,768]{1,0:T(8,128)(2,1)}, u32[]{:S(2)}, u32[]{:S(2)}) collective-permute-start(bf16[768,768]{1,0:T(8,128)(2,1)} %refs_8_.5), channel_id=1, source_target_pairs={{0,1},{1,0},{2,3},{3,2},{4,5},{5,4},{6,7},{7,6},{8,9},{9,8},{10,11... | collective-permute-start | bytes 3538952 | tf_op jit(solution)/shard_map/ppermute | solution.py:823
  9.4 29.8 %collective-permute-start.6 = (bf16[16,768]{1,0:T(8,128)(2,1)S(1)}, bf16[16,768]{1,0:T(8,128)(2,1)S(1)}, u32[]{:S(2)}, u32[]{:S(2)}) collective-permute-start(bf16[16,768]{1,0:T(8,128)(2,1)S(1)} %pad.4.refs_11_), channel_id=1, source_target_pairs={{0,1},{1,0},{2,3},{3,2},{4,5},{5,4},{6,7},{7,6},{8,9},{9,8},{10,11... | collective-permute-start | bytes 73736 | tf_op jit(solution)/shard_map/ppermute | solution.py:823
  39.2 31.3 %copy-start.19 = (bf16[16,768]{1,0:T(8,128)(2,1)}, bf16[16,768]{1,0:T(8,128)(2,1)S(1)}, u32[]{:S(2)}) copy-start(bf16[16,768]{1,0:T(8,128)(2,1)S(1)} %collective-permute-done.6.refs_12_) | copy-start | bytes 73732
  39.2 1.9 collective-permute-start.7
  39.7 9.4 %collective-permute-start.8 = (bf16[512,192]{1,0:T(8,128)(2,1)}, bf16[512,192]{1,0:T(8,128)(2,1)S(1)}, u32[]{:S(2)}, u32[]{:S(2)}) collective-permute-start(bf16[512,192]{1,0:T(8,128)(2,1)} %get-tuple-element.144), channel_id=1, source_target_pairs={{0,2},{1,3},{2,0},{3,1},{4,6},{5,7},{6,4},{7,5},{8,10},{9,11},{10,... | collective-permute-start | bytes 589832 | tf_op jit(solution)/shard_map/ppermute | solution.py:823
  40.0 12.9 %collective-permute-start.9 = (bf16[512,192]{1,0:T(8,128)(2,1)}, bf16[512,192]{1,0:T(8,128)(2,1)S(1)}, u32[]{:S(2)}, u32[]{:S(2)}) collective-permute-start(bf16[512,192]{1,0:T(8,128)(2,1)} %get-tuple-element.145), channel_id=1, source_target_pairs={{0,3},{1,2},{2,1},{3,0},{4,7},{5,6},{6,5},{7,4},{8,11},{9,10},{10,... | collective-permute-start | bytes 589832 | tf_op jit(solution)/shard_map/ppermute | solution.py:823
  53.0 49.7 %collective-permute-start.11 = (bf16[784,768]{1,0:T(8,128)(2,1)}, bf16[784,768]{1,0:T(8,128)(2,1)S(1)}, u32[]{:S(2)}, u32[]{:S(2)}) collective-permute-start(bf16[784,768]{1,0:T(8,128)(2,1)} %collective-permute-done.3.refs_13_), channel_id=1, source_target_pairs={{0,4},{4,0},{8,12},{12,8},{16,20},{20,16},{24,28},{28,24},{1,5},{5... | collective-permute-start | bytes 3612680 | tf_op jit(solution)/shard_map/ppermute | solution.py:823
  54.5 16.0 %collective-permute-start.12 = (bf16[512,192]{1,0:T(8,128)(2,1)}, bf16[512,192]{1,0:T(8,128)(2,1)S(1)}, u32[]{:S(2)}, u32[]{:S(2)}) collective-permute-start(bf16[512,192]{1,0:T(8,128)(2,1)} %get-tuple-element.156), channel_id=1, source_target_pairs={{0,1},{1,0},{2,3},{3,2},{4,5},{5,4},{6,7},{7,6},{8,9},{9,8},{10,11... | collective-permute-start | bytes 589832 | tf_op jit(solution)/shard_map/ppermute | solution.py:823
  54.9 15.6 %collective-permute-start.13 = (bf16[512,192]{1,0:T(8,128)(2,1)}, bf16[512,192]{1,0:T(8,128)(2,1)S(1)}, u32[]{:S(2)}, u32[]{:S(2)}) collective-permute-start(bf16[512,192]{1,0:T(8,128)(2,1)} %get-tuple-element.157), channel_id=1, source_target_pairs={{0,2},{1,3},{2,0},{3,1},{4,6},{5,7},{6,4},{7,5},{8,10},{9,11},{10,... | collective-permute-start | bytes 589832 | tf_op jit(solution)/shard_map/ppermute | solution.py:823
  55.4 15.1 %collective-permute-start.14 = (bf16[512,192]{1,0:T(8,128)(2,1)}, bf16[512,192]{1,0:T(8,128)(2,1)S(1)}, u32[]{:S(2)}, u32[]{:S(2)}) collective-permute-start(bf16[512,192]{1,0:T(8,128)(2,1)} %get-tuple-element.158), channel_id=1, source_target_pairs={{0,3},{1,2},{2,1},{3,0},{4,7},{5,6},{6,5},{7,4},{8,11},{9,10},{10,... | collective-permute-start | bytes 589832 | tf_op jit(solution)/shard_map/ppermute | solution.py:823
  70.5 16.5 %copy-start.25 = (bf16[512,192]{1,0:T(8,128)(2,1)S(1)}, bf16[512,192]{1,0:T(8,128)(2,1)}, u32[]{:S(2)}) copy-start(bf16[512,192]{1,0:T(8,128)(2,1)} %get-tuple-element.180) | copy-start | bytes 589828
  70.5 17.1 %copy-start.24 = (bf16[512,192]{1,0:T(8,128)(2,1)S(1)}, bf16[512,192]{1,0:T(8,128)(2,1)}, u32[]{:S(2)}) copy-start(bf16[512,192]{1,0:T(8,128)(2,1)} %get-tuple-element.181) | copy-start | bytes 589828
  70.6 15.7 %collective-permute-start.15 = (bf16[512,192]{1,0:T(8,128)(2,1)S(1)}, bf16[512,192]{1,0:T(8,128)(2,1)S(1)}, u32[]{:S(2)}, u32[]{:S(2)}) collective-permute-start(bf16[512,192]{1,0:T(8,128)(2,1)S(1)} %copy-done.29), channel_id=1, source_target_pairs={{0,1},{1,0},{2,3},{3,2},{4,5},{5,4},{6,7},{7,6},{8,9},{9,8},{10,11... | collective-permute-start | bytes 589832 | tf_op jit(solution)/shard_map/ppermute | solution.py:823
  71.3 14.9 %collective-permute-start.16 = (bf16[512,192]{1,0:T(8,128)(2,1)S(1)}, bf16[512,192]{1,0:T(8,128)(2,1)S(1)}, u32[]{:S(2)}, u32[]{:S(2)}) collective-permute-start(bf16[512,192]{1,0:T(8,128)(2,1)S(1)} %copy-done.28), channel_id=1, source_target_pairs={{0,2},{1,3},{2,0},{3,1},{4,6},{5,7},{6,4},{7,5},{8,10},{9,11},{10,... | collective-permute-start | bytes 589832 | tf_op jit(solution)/shard_map/ppermute | solution.py:823
  71.9 14.4 %collective-permute-start.17 = (bf16[512,192]{1,0:T(8,128)(2,1)S(1)}, bf16[512,192]{1,0:T(8,128)(2,1)S(1)}, u32[]{:S(2)}, u32[]{:S(2)}) collective-permute-start(bf16[512,192]{1,0:T(8,128)(2,1)S(1)} %copy-done.27), channel_id=1, source_target_pairs={{0,3},{1,2},{2,1},{3,0},{4,7},{5,6},{6,5},{7,4},{8,11},{9,10},{10,... | collective-permute-start | bytes 589832 | tf_op jit(solution)/shard_map/ppermute | solution.py:823
  86.3 16.3 %collective-permute-start.18 = (bf16[512,192]{1,0:T(8,128)(2,1)S(1)}, bf16[512,192]{1,0:T(8,128)(2,1)S(1)}, u32[]{:S(2)}, u32[]{:S(2)}) collective-permute-start(bf16[512,192]{1,0:T(8,128)(2,1)S(1)} %copy-done.26), channel_id=1, source_target_pairs={{0,1},{1,0},{2,3},{3,2},{4,5},{5,4},{6,7},{7,6},{8,9},{9,8},{10,11... | collective-permute-start | bytes 589832 | tf_op jit(solution)/shard_map/ppermute | solution.py:823
  87.1 15.5 %collective-permute-start.19 = (bf16[512,192]{1,0:T(8,128)(2,1)S(1)}, bf16[512,192]{1,0:T(8,128)(2,1)S(1)}, u32[]{:S(2)}, u32[]{:S(2)}) collective-permute-start(bf16[512,192]{1,0:T(8,128)(2,1)S(1)} %copy-done.25), channel_id=1, source_target_pairs={{0,2},{1,3},{2,0},{3,1},{4,6},{5,7},{6,4},{7,5},{8,10},{9,11},{10,... | collective-permute-start | bytes 589832 | tf_op jit(solution)/shard_map/ppermute | solution.py:823
  87.6 15.0 %collective-permute-start.20 = (bf16[512,192]{1,0:T(8,128)(2,1)S(1)}, bf16[512,192]{1,0:T(8,128)(2,1)S(1)}, u32[]{:S(2)}, u32[]{:S(2)}) collective-permute-start(bf16[512,192]{1,0:T(8,128)(2,1)S(1)} %copy-done.24), channel_id=1, source_target_pairs={{0,3},{1,2},{2,1},{3,0},{4,7},{5,6},{6,5},{7,4},{8,11},{9,10},{10,... | collective-permute-start | bytes 589832 | tf_op jit(solution)/shard_map/ppermute | solution.py:823
  88.5 28.1 %collective-permute-start.10 = (bf16[784,768]{1,0:T(8,128)(2,1)}, bf16[784,768]{1,0:T(8,128)(2,1)S(1)}, u32[]{:S(2)}, u32[]{:S(2)}) collective-permute-start(bf16[784,768]{1,0:T(8,128)(2,1)} %collective-permute-done.3.refs_13_), channel_id=1, source_target_pairs={{0,1},{1,0},{2,3},{3,2},{4,5},{5,4},{6,7},{7,6},{8,9},{9,8},{10,11... | collective-permute-start | bytes 3612680 | tf_op jit(solution)/shard_map/ppermute | solution.py:823
  102.6 14.0 %collective-permute-start.21 = (bf16[784,768]{1,0:T(8,128)(2,1)S(1)}, bf16[784,768]{1,0:T(8,128)(2,1)S(1)}, u32[]{:S(2)}, u32[]{:S(2)}) collective-permute-start(bf16[784,768]{1,0:T(8,128)(2,1)S(1)} %collective-permute-done.11.refs_15_), channel_id=1, source_target_pairs={{0,1},{1,0},{2,3},{3,2},{4,5},{5,4},{6,7},{7,6},{8,9},{9,8},{10,11... | collective-permute-start | bytes 3612680 | tf_op jit(solution)/shard_map/ppermute | solution.py:823
  192.3 1.5 collective-permute-start.22
  194.7 4.4 %collective-permute-start.23 = (f32[24,768]{1,0:T(8,128)S(1)}, f32[24,768]{1,0:T(8,128)S(1)}, u32[]{:S(2)}, u32[]{:S(2)}) collective-permute-start(f32[24,768]{1,0:T(8,128)S(1)} %add.19), channel_id=1, source_target_pairs={{0,2},{1,3},{2,0},{3,1},{4,6},{5,7},{6,4},{7,5},{8,10},{9,11},{10,... | collective-permute-start | bytes 221192 | tf_op jit(solution)/shard_map/ppermute | solution.py:823
  199.2 4.4 %collective-permute-start.24 = (f32[24,768]{1,0:T(8,128)S(1)}, f32[24,768]{1,0:T(8,128)S(1)}, u32[]{:S(2)}, u32[]{:S(2)}) collective-permute-start(f32[24,768]{1,0:T(8,128)S(1)} %add.20), channel_id=1, source_target_pairs={{0,4},{4,0},{8,12},{12,8},{16,20},{20,16},{24,28},{28,24},{1,5},{5... | collective-permute-start | bytes 221192 | tf_op jit(solution)/shard_map/ppermute | solution.py:823
  203.6 4.4 %collective-permute-start.25 = (f32[24,768]{1,0:T(8,128)S(1)}, f32[24,768]{1,0:T(8,128)S(1)}, u32[]{:S(2)}, u32[]{:S(2)}) collective-permute-start(f32[24,768]{1,0:T(8,128)S(1)} %add.21), channel_id=1, source_target_pairs={{0,8},{4,12},{8,0},{12,4},{16,24},{20,28},{24,16},{28,20},{1,9},{5... | collective-permute-start | bytes 221192 | tf_op jit(solution)/shard_map/ppermute | solution.py:823
  208.0 6.5 %collective-permute-start.26 = (f32[24,768]{1,0:T(8,128)S(1)}, f32[24,768]{1,0:T(8,128)S(1)}, u32[]{:S(2)}, u32[]{:S(2)}) collective-permute-start(f32[24,768]{1,0:T(8,128)S(1)} %add.22.acc_ref), channel_id=1, source_target_pairs={{0,16},{4,20},{8,24},{12,28},{16,0},{20,4},{24,8},{28,12},{1,17},{... | collective-permute-start | bytes 221192 | tf_op jit(solution)/shard_map/ppermute | solution.py:823
  (25 other events, 142.8 us)
where the time goes:
time: 224 us; the launch traced here: 220 us
  Pallas kernels  161 us (72%)
  waiting for transfers between devices  26.9 us (12%)
  starting transfers between devices  22.3 us (10%)
  local copies, waits for them, and re-layouts  6.47 us (3%)
    pallas_call x1, Pallas kernels, finish_call(): pl.pallas_call(functools.partial(finish_kernel, plan=plan, arrays=len(arr...  73.6 us
    pallas_call x4, Pallas kernels, attend_call(): pl.pallas_call(functools.partial(attend_kernel, parts=parts, unit=unit, f...  53 us
    pallas_call x1, Pallas kernels, embed_call(): pl.pallas_call(functools.partial(embed_kernel, parts=parts, units=units),...  29.7 us
    ppermute x27, waiting for transfers between devices, swap(): return lax.ppermute(value, axis, [(i, i ^ bit) for i in range(size)])  26.9 us
    ppermute x27, starting transfers between devices, swap(): return lax.ppermute(value, axis, [(i, i ^ bit) for i in range(size)])  22.3 us
    pallas_call x1, Pallas kernels, update_call(): pl.pallas_call(update_kernel, out_shape=[one, one, one, flat, flat, jax.S...  4.67 us
  transfers between devices with their start and end apart: 27, of which 7 were waited for; matrix products, arithmetic and copies ran while one was open for 2% of the time, Pallas kernels for 38%

commit v1 on v0

--- a/solution.py
+++ b/solution.py
@@ -35,6 +35,7 @@
 RING = 6
 UNROLL = 64
 ACC_ROWS = 24
+ADAPTER_ROWS = 16
 BIAS_ROWS = 16
 MIB = 1024 * 1024
 NN = (((1,), (0,)), ((), ()))
@@ -282,7 +283,7 @@
     rank = up_ref.shape[1]
     spot = lax.broadcasted_iota(jnp.int32, (rank, GROUP), 1) % HEAD_DIM
     line = lax.broadcasted_iota(jnp.int32, (rank, GROUP), 0)
-    lows = [mm(xb[...], down_ref[i]).astype(BF16) for i in range(2)]
+    lows = [mm(xb[...], down_ref[i], NT).astype(BF16) for i in range(2)]
     ups = [up_ref[i].astype(BF16) * BF16(2.0) for i in range(2)]
     red[...] = add_all(
         [
@@ -441,7 +442,7 @@
     seg_ref, label_ref, gain_ref, shift_ref, bias_ref, head_ref, wo_hbm, *refs = refs
     weight_refs, refs = refs[:arrays], refs[arrays:]
     kept, refs = refs[:6], refs[6:]
-    acc_ref, refs = refs[0], refs[1:]
+    packed_ref, acc_ref, refs = refs[0], refs[1], refs[2:]
     bufs, refs = (refs[:6], refs[6:12]), refs[12:]
     xbs, xh1s, stats, refs = refs[:3], refs[3:6], refs[6:9], refs[9:]
     accs, slopes, acts, refs = refs[:2], refs[2:4], refs[4:6], refs[6:]
@@ -695,13 +696,30 @@
         interleave(feed_back(u), norm1(u + 2) if u + 2 < units else [])
         interleave(attention_back(u), feed_out(u + 1) if later else [])
 
+    slabs = width // LANES
+    for j in range(slabs):
+        lanes = slice(j * LANES, (j + 1) * LANES)
+        packed_ref[j * ADAPTER_ROWS : (j + 1) * ADAPTER_ROWS, :] = acc_ref[0:ADAPTER_ROWS, lanes]
+    rest = [acc_ref[16:17, j * LANES : (j + 1) * LANES] for j in range(slabs)]
+    rest.append(acc_ref[17:18, 0:LANES])
+    empty = packed_ref.shape[0] - slabs * ADAPTER_ROWS - len(rest)
+    if empty:
+        rest.append(jnp.zeros((empty, LANES), F32))
+    packed_ref[slabs * ADAPTER_ROWS :, :] = jnp.concatenate(rest, axis=0)
+
+
+def packed_rows(width):
+    slabs = width // LANES
+    return pl.cdiv(slabs * ADAPTER_ROWS + slabs + 1, 8) * 8
+
 
 def finish_call(segs, labels, small, wo, arrays, plan, kept, parts):
     gain, shift, bias, head = small
     units, rows, width = kept[0].shape
     hidden_part = arrays[0].shape[1]
     hidden = hidden_part * parts
-    scratch = [pltpu.VMEM(a.shape[1:], a.dtype) for a in kept] * 2
+    scratch = [pltpu.VMEM((ACC_ROWS, width), F32)]
+    scratch += [pltpu.VMEM(a.shape[1:], a.dtype) for a in kept] * 2
     scratch += [pltpu.VMEM((rows, width), BF16)] * 3
     scratch += [pltpu.VMEM((rows, width), F32)] * 3
     scratch += [pltpu.VMEM((rows, 1), F32)] * 3
@@ -718,7 +736,7 @@
     ]
     return pl.pallas_call(
         functools.partial(finish_kernel, plan=plan, arrays=len(arrays), parts=parts),
-        out_shape=jax.ShapeDtypeStruct((ACC_ROWS, width), F32),
+        out_shape=jax.ShapeDtypeStruct((packed_rows(width), LANES), F32),
         in_specs=[VMEM] * 6 + [ANY] * (1 + len(arrays) + len(kept)),
         out_specs=VMEM,
         scratch_shapes=scratch,
@@ -747,13 +765,22 @@
     head_low_out,
 ):
     total = acc_ref[...] + other_ref[...]
-    width = total.shape[1]
+    width = up_ref.shape[1]
     rank = up_ref.shape[0] // 2
-    items = total[17:18, 1:2]
-    loss_ref[...] = total[17:18, 0:1]
+    slabs = width // LANES
+    top = slabs * ADAPTER_ROWS
+    sums = total[top + slabs : top + slabs + 1]
+    items = sums[:, 1:2]
+    loss_ref[...] = sums[:, 0:1]
     items_ref[...] = items
-    adapter = total[0:16] / items
-    head_grad = jnp.concatenate([total[16:17], total[17:18, 2:3]], axis=1) / items
+    adapter = (
+        jnp.concatenate(
+            [total[j * ADAPTER_ROWS : (j + 1) * ADAPTER_ROWS] for j in range(slabs)], axis=1
+        )
+        / items
+    )
+    head_grad = [total[top + j : top + j + 1] for j in range(slabs)] + [sums[:, 2:3]]
+    head_grad = jnp.concatenate(head_grad, axis=1) / items
     norm = jnp.sqrt(jnp.sum(adapter * adapter) + jnp.sum(head_grad * head_grad))
     norm_ref[...] = jnp.full((1, 1), norm, F32)
     factor = jnp.minimum(1.0, CLIP_NORM / (norm_ref[...] + 1e-06))
@@ -938,7 +965,7 @@
         norm_gain_rows,
         norm_shift_rows,
         attention_bias_stack,
-        adapter_down_weight,
+        jnp.swapaxes(adapter_down_weight, 1, 2),
         adapter_up_weight,
     )
     kept = None

time: 224 us -> 220 us (0.982)
  transfers between devices with their start and end apart: 27 -> 27, of which waited for: 7 -> 7; matrix products, arithmetic and copies ran while one was open for 2% -> 1% of each run, Pallas kernels for 38% -> 38%
where the time goes in v1:
time: 220 us; the launch traced here: 216 us
  Pallas kernels  160 us (73%)
  waiting for transfers between devices  25.2 us (11%)
  starting transfers between devices  21.9 us (10%)
  local copies, waits for them, and re-layouts  5.61 us (3%)
    pallas_call x1, Pallas kernels, finish_call(): pl.pallas_call(functools.partial(finish_kernel, plan=plan, arrays=len(arr...  73.1 us
    pallas_call x4, Pallas kernels, attend_call(): pl.pallas_call(functools.partial(attend_kernel, parts=parts, unit=unit, f...  52.2 us
    pallas_call x1, Pallas kernels, embed_call(): pl.pallas_call(functools.partial(embed_kernel, parts=parts, units=units),...  29.7 us
    ppermute x27, waiting for transfers between devices, swap(): return lax.ppermute(value, axis, [(i, i ^ bit) for i in range(size)])  25.2 us
    ppermute x27, starting transfers between devices, swap(): return lax.ppermute(value, axis, [(i, i ^ bit) for i in range(size)])  21.9 us
    pallas_call x1, Pallas kernels, update_call(): pl.pallas_call(update_kernel, out_shape=[one, one, one, flat, flat, jax.S...  4.6 us
  transfers between devices with their start and end apart: 27, of which 7 were waited for; matrix products, arithmetic and copies ran while one was open for 1% of the time, Pallas kernels for 38%

profile of v1, /device:TPU:0, one launch (start us, length us, event | category | flops | bytes accessed | tf_op | source)
XLA Modules:
  0.0 215.7 jit_solution(15695067340568217123)
XLA Ops:
  1.2 2.6 %collective-permute-start.1 = (s32[4,1,512]{2,1,0:T(1,128)}, s32[4,1,512]{2,1,0:T(1,128)S(1)}, u32[]{:S(2)}, u32[]{:S(2)}) collective-permute-start(s32[4,1,512]{2,1,0:T(1,128)} %refs_0_.1), channel_id=1, source_target_pairs={{0,2},{1,3},{2,0},{3,1},{4,6},{5,7},{6,4},{7,5},{8,10},{9,11},{10,... | collective-permute-start | bytes 24584 | tf_op jit(solution)/shard_map/ppermute | solution.py:850
  3.8 0.7 broadcast_in_dim.3
  4.5 1.3 constant_dynamic-slice_fusion
  5.8 1.2 pad_maximum_fusion
  7.0 1.8 collective-permute-start.3
  9.4 29.7 %embed.1 = (bf16[512,192]{1,0:T(8,128)(2,1)}, bf16[512,192]{1,0:T(8,128)(2,1)}, bf16[512,192]{1,0:T(8,128)(2,1)}, bf16[512,192]{1,0:T(8,128)(2,1)}, bf16[512,192...) custom-call(s32[4,1,512]{2,1,0:T(1,128)} %refs_0_.1, ...), custom_call_target="tpu_custom_call" | custom-call | tf_op jit(solution)/shard_map/embed/pallas_call | solution.py:148
  40.0 1.1 collective-permute-start.9
  41.2 7.9 %collective-permute-done.8.refs_2_ = bf16[512,192]{1,0:T(8,128)(2,1)S(1)} collective-permute-done((bf16[512,192]{1,0:T(8,128)(2,1)}, bf16[512,192]{1,0:T(8,128)(2,1)S(1)}, u32[]{:S(2)}, u32[]{:S(2)}) %collective-permute-start.8) | collective-permute-done | bytes 196640 | tf_op jit(solution)/shard_map/ppermute | solution.py:850
  49.1 3.9 %collective-permute-done.9.refs_3_ = bf16[512,192]{1,0:T(8,128)(2,1)S(1)} collective-permute-done((bf16[512,192]{1,0:T(8,128)(2,1)}, bf16[512,192]{1,0:T(8,128)(2,1)S(1)}, u32[]{:S(2)}, u32[]{:S(2)}) %collective-permute-start.9) | collective-permute-done | bytes 196640 | tf_op jit(solution)/shard_map/ppermute | solution.py:850
  53.0 1.5 collective-permute-start.11
  55.4 0.9 collective-permute-start.14
  56.4 13.0 %attend.4 = (f32[4,512,768]{2,1,0:T(8,128)}, bf16[4,512,768]{2,1,0:T(8,128)(2,1)}, bf16[4,512,768]{2,1,0:T(8,128)(2,1)}, bf16[4,512,256]{2,1,0:T(8,128)(2,1)}, b...) custom-call(bf16[512,192]{1,0:T(8,128)(2,1)} %get-tuple-element.159.refs_0_, ...), custom_call_target="tpu_custom_call" | custom-call | flops 393216 | bytes 262144 | tf_op jit(solution)/shard_map/attend/pallas_call | solution.py:424
  69.5 0.8 collective-permute-start.15
  70.8 0.9 collective-permute-start.17
  71.7 13.2 %attend.5 = (f32[4,512,768]{2,1,0:T(8,128)}, bf16[4,512,768]{2,1,0:T(8,128)(2,1)}, bf16[4,512,768]{2,1,0:T(8,128)(2,1)}, bf16[4,512,256]{2,1,0:T(8,128)(2,1)}, b...) custom-call(bf16[512,192]{1,0:T(8,128)(2,1)} %get-tuple-element.172., ...), custom_call_target="tpu_custom_call", output_to_operand_aliasing={{0}: (13, {}), {1}: (14, {}), {2}: (15, {}), {3}: (16, {}),... | custom-call | flops 393216 | bytes 262144 | tf_op jit(solution)/shard_map/attend/pallas_call | solution.py:424
  84.9 0.8 collective-permute-start.18
  86.2 0.9 collective-permute-start.20
  87.2 0.7 collective-permute-start.10
  87.9 13.1 %attend.6 = (f32[4,512,768]{2,1,0:T(8,128)}, bf16[4,512,768]{2,1,0:T(8,128)(2,1)}, bf16[4,512,768]{2,1,0:T(8,128)(2,1)}, bf16[4,512,256]{2,1,0:T(8,128)(2,1)}, b...) custom-call(bf16[512,192]{1,0:T(8,128)(2,1)} %get-tuple-element.182., ...), custom_call_target="tpu_custom_call", output_to_operand_aliasing={{0}: (13, {}), {1}: (14, {}), {2}: (15, {}), {3}: (16, {}),... | custom-call | flops 393216 | bytes 262144 | tf_op jit(solution)/shard_map/attend/pallas_call | solution.py:424
  102.0 12.9 %attend.7 = (f32[4,512,768]{2,1,0:T(8,128)}, bf16[4,512,768]{2,1,0:T(8,128)(2,1)}, bf16[4,512,768]{2,1,0:T(8,128)(2,1)}, bf16[4,512,256]{2,1,0:T(8,128)(2,1)}, b...) custom-call(bf16[512,192]{1,0:T(8,128)(2,1)} %get-tuple-element.190., ...), custom_call_target="tpu_custom_call", output_to_operand_aliasing={{0}: (13, {}), {1}: (14, {}), {2}: (15, {}), {3}: (16, {}),... | custom-call | flops 393216 | bytes 262144 | tf_op jit(solution)/shard_map/attend/pallas_call | solution.py:424
  114.9 1.0 copy-done.2
  115.9 1.1 copy-done.3
  117.0 73.1 %finish.1 = f32[104,128]{1,0:T(8,128)} custom-call(s32[4,1,512]{2,1,0:T(1,128)} %refs_0_.2, f32[4,1,64]{2,1,0:T(1,128)} %refs_1_.1, f32[3,768]{1,0:T(4,128)} %refs_2_.1, f32[3,768]{1,0:T(4,128)} %refs_3_.1, f32[5,768]{1,0:T(8,128)} %refs_4_.11, f32[769]{0:T(1024)} %head_ref, bf16[768,768]{1,0:T(8,128)(2,1)} %refs_6_.9, bf16[768,768]{1,0:T(8,128)(2,1)} %refs_7_.9, ...), custom_call_target="tpu_custom_call" | custom-call | tf_op jit(solution)/shard_map/finish/pallas_call | solution.py:737
  190.2 1.4 collective-permute-done.22
  191.7 0.8 add.19
  193.0 3.6 %collective-permute-done.23 = f32[104,128]{1,0:T(8,128)S(1)} collective-permute-done((f32[104,128]{1,0:T(8,128)S(1)}, f32[104,128]{1,0:T(8,128)S(1)}, u32[]{:S(2)}, u32[]{:S(2)}) %collective-permute-start.23) | collective-permute-done | bytes 53280 | tf_op jit(solution)/shard_map/ppermute | solution.py:850
  197.2 3.6 %collective-permute-done.24 = f32[104,128]{1,0:T(8,128)S(1)} collective-permute-done((f32[104,128]{1,0:T(8,128)S(1)}, f32[104,128]{1,0:T(8,128)S(1)}, u32[]{:S(2)}, u32[]{:S(2)}) %collective-permute-start.24) | collective-permute-done | bytes 53280 | tf_op jit(solution)/shard_map/ppermute | solution.py:850
  200.8 1.7 collective-permute-start.25
  202.5 2.5 %collective-permute-done.25 = f32[104,128]{1,0:T(8,128)S(1)} collective-permute-done((f32[104,128]{1,0:T(8,128)S(1)}, f32[104,128]{1,0:T(8,128)S(1)}, u32[]{:S(2)}, u32[]{:S(2)}) %collective-permute-start.25) | collective-permute-done | bytes 53280 | tf_op jit(solution)/shard_map/ppermute | solution.py:850
  205.1 3.1 %collective-permute-start.26 = (f32[104,128]{1,0:T(8,128)S(1)}, f32[104,128]{1,0:T(8,128)S(1)}, u32[]{:S(2)}, u32[]{:S(2)}) collective-permute-start(f32[104,128]{1,0:T(8,128)S(1)} %add.22.acc_ref), channel_id=1, source_target_pairs={{0,16},{4,20},{8,24},{12,28},{16,0},{20,4},{24,8},{28,12},{1,17},{... | collective-permute-start | bytes 159752 | tf_op jit(solution)/shard_map/ppermute | solution.py:850
  208.1 2.1 collective-permute-done.26.other_ref
  210.9 4.6 %update.1 = (f32[1,1]{1,0:T(1,128)}, f32[1,1]{1,0:T(1,128)}, f32[1,1]{1,0:T(1,128)}, f32[16,768]{1,0:T(8,128)}, f32[16,768]{1,0:T(8,128)}, /*index=5*/bf16[16,76...) custom-call(f32[104,128]{1,0:T(8,128)} %copy-done.17, f32[104,128]{1,0:T(8,128)} %copy-done.18, ...), custom_call_target="tpu_custom_call" | custom-call | tf_op jit(solution)/shard_map/update/pallas_call | solution.py:828
  (95 shorter events, 6.8 us)
Async XLA Ops:
  0.7 6.3 %collective-permute-start = (s32[4,1,512]{2,1,0:T(1,128)}, s32[4,1,512]{2,1,0:T(1,128)S(1)}, u32[]{:S(2)}, u32[]{:S(2)}) collective-permute-start(s32[4,1,512]{2,1,0:T(1,128)} %refs_0_.1), channel_id=1, source_target_pairs={{0,1},{1,0},{2,3},{3,2},{4,5},{5,4},{6,7},{7,6},{8,9},{9,8},{10,11... | collective-permute-start | bytes 24584 | tf_op jit(solution)/shard_map/ppermute | solution.py:850
  1.2 5.8 %collective-permute-start.1 = (s32[4,1,512]{2,1,0:T(1,128)}, s32[4,1,512]{2,1,0:T(1,128)S(1)}, u32[]{:S(2)}, u32[]{:S(2)}) collective-permute-start(s32[4,1,512]{2,1,0:T(1,128)} %refs_0_.1), channel_id=1, source_target_pairs={{0,2},{1,3},{2,0},{3,1},{4,6},{5,7},{6,4},{7,5},{8,10},{9,11},{10,... | collective-permute-start | bytes 24584 | tf_op jit(solution)/shard_map/ppermute | solution.py:850
  3.7 3.3 %collective-permute-start.2 = (s32[4,1,512]{2,1,0:T(1,128)}, s32[4,1,512]{2,1,0:T(1,128)S(1)}, u32[]{:S(2)}, u32[]{:S(2)}) collective-permute-start(s32[4,1,512]{2,1,0:T(1,128)} %refs_0_.1), channel_id=1, source_target_pairs={{0,3},{1,2},{2,1},{3,0},{4,7},{5,6},{6,5},{7,4},{8,11},{9,10},{10,... | collective-permute-start | bytes 24584 | tf_op jit(solution)/shard_map/ppermute | solution.py:850
  4.5 34.7 %copy-start.16 = (bf16[16,768]{1,0:T(8,128)(2,1)}, bf16[16,768]{1,0:T(8,128)(2,1)S(1)}, u32[]{:S(2)}) copy-start(bf16[16,768]{1,0:T(8,128)(2,1)S(1)} %pad.4.refs_11_) | copy-start | bytes 73732
  7.0 32.2 %collective-permute-start.3 = (bf16[784,768]{1,0:T(8,128)(2,1)}, bf16[784,768]{1,0:T(8,128)(2,1)}, u32[]{:S(2)}, u32[]{:S(2)}) collective-permute-start(bf16[784,768]{1,0:T(8,128)(2,1)} %pad_maximum_fusion), channel_id=1, source_target_pairs={{0,2},{1,3},{2,0},{3,1},{4,6},{5,7},{6,4},{7,5},{8,10},{9,11},{10,... | collective-permute-start | bytes 3612680 | tf_op jit(solution)/shard_map/ppermute | solution.py:850
  8.8 30.4 %collective-permute-start.4 = (bf16[768,768]{1,0:T(8,128)(2,1)S(1)}, bf16[768,768]{1,0:T(8,128)(2,1)}, u32[]{:S(2)}, u32[]{:S(2)}) collective-permute-start(bf16[768,768]{1,0:T(8,128)(2,1)S(1)} %copy-done), channel_id=1, source_target_pairs={{0,1},{1,0},{2,3},{3,2},{4,5},{5,4},{6,7},{7,6},{8,9},{9,8},{10,11... | collective-permute-start | bytes 3538952 | tf_op jit(solution)/shard_map/ppermute | solution.py:850
  8.9 30.3 %collective-permute-start.5 = (bf16[768,768]{1,0:T(8,128)(2,1)}, bf16[768,768]{1,0:T(8,128)(2,1)}, u32[]{:S(2)}, u32[]{:S(2)}) collective-permute-start(bf16[768,768]{1,0:T(8,128)(2,1)} %refs_8_.1), channel_id=1, source_target_pairs={{0,1},{1,0},{2,3},{3,2},{4,5},{5,4},{6,7},{7,6},{8,9},{9,8},{10,11... | collective-permute-start | bytes 3538952 | tf_op jit(solution)/shard_map/ppermute | solution.py:850
  9.3 29.8 %collective-permute-start.6 = (bf16[16,768]{1,0:T(8,128)(2,1)S(1)}, bf16[16,768]{1,0:T(8,128)(2,1)S(1)}, u32[]{:S(2)}, u32[]{:S(2)}) collective-permute-start(bf16[16,768]{1,0:T(8,128)(2,1)S(1)} %pad.4.refs_11_), channel_id=1, source_target_pairs={{0,1},{1,0},{2,3},{3,2},{4,5},{5,4},{6,7},{7,6},{8,9},{9,8},{10,11... | collective-permute-start | bytes 73736 | tf_op jit(solution)/shard_map/ppermute | solution.py:850
  39.2 30.2 %copy-start.19 = (bf16[16,768]{1,0:T(8,128)(2,1)}, bf16[16,768]{1,0:T(8,128)(2,1)S(1)}, u32[]{:S(2)}) copy-start(bf16[16,768]{1,0:T(8,128)(2,1)S(1)} %collective-permute-done.6.refs_12_) | copy-start | bytes 73732
  39.2 1.9 collective-permute-start.7
  39.7 9.4 %collective-permute-start.8 = (bf16[512,192]{1,0:T(8,128)(2,1)}, bf16[512,192]{1,0:T(8,128)(2,1)S(1)}, u32[]{:S(2)}, u32[]{:S(2)}) collective-permute-start(bf16[512,192]{1,0:T(8,128)(2,1)} %get-tuple-element.144), channel_id=1, source_target_pairs={{0,2},{1,3},{2,0},{3,1},{4,6},{5,7},{6,4},{7,5},{8,10},{9,11},{10,... | collective-permute-start | bytes 589832 | tf_op jit(solution)/shard_map/ppermute | solution.py:850
  40.0 12.9 %collective-permute-start.9 = (bf16[512,192]{1,0:T(8,128)(2,1)}, bf16[512,192]{1,0:T(8,128)(2,1)S(1)}, u32[]{:S(2)}, u32[]{:S(2)}) collective-permute-start(bf16[512,192]{1,0:T(8,128)(2,1)} %get-tuple-element.145), channel_id=1, source_target_pairs={{0,3},{1,2},{2,1},{3,0},{4,7},{5,6},{6,5},{7,4},{8,11},{9,10},{10,... | collective-permute-start | bytes 589832 | tf_op jit(solution)/shard_map/ppermute | solution.py:850
  53.0 48.1 %collective-permute-start.11 = (bf16[784,768]{1,0:T(8,128)(2,1)}, bf16[784,768]{1,0:T(8,128)(2,1)S(1)}, u32[]{:S(2)}, u32[]{:S(2)}) collective-permute-start(bf16[784,768]{1,0:T(8,128)(2,1)} %collective-permute-done.3.refs_13_), channel_id=1, source_target_pairs={{0,4},{4,0},{8,12},{12,8},{16,20},{20,16},{24,28},{28,24},{1,5},{5... | collective-permute-start | bytes 3612680 | tf_op jit(solution)/shard_map/ppermute | solution.py:850
  54.5 14.9 %collective-permute-start.12 = (bf16[512,192]{1,0:T(8,128)(2,1)}, bf16[512,192]{1,0:T(8,128)(2,1)S(1)}, u32[]{:S(2)}, u32[]{:S(2)}) collective-permute-start(bf16[512,192]{1,0:T(8,128)(2,1)} %get-tuple-element.156), channel_id=1, source_target_pairs={{0,1},{1,0},{2,3},{3,2},{4,5},{5,4},{6,7},{7,6},{8,9},{9,8},{10,11... | collective-permute-start | bytes 589832 | tf_op jit(solution)/shard_map/ppermute | solution.py:850
  54.9 14.5 %collective-permute-start.13 = (bf16[512,192]{1,0:T(8,128)(2,1)}, bf16[512,192]{1,0:T(8,128)(2,1)S(1)}, u32[]{:S(2)}, u32[]{:S(2)}) collective-permute-start(bf16[512,192]{1,0:T(8,128)(2,1)} %get-tuple-element.157), channel_id=1, source_target_pairs={{0,2},{1,3},{2,0},{3,1},{4,6},{5,7},{6,4},{7,5},{8,10},{9,11},{10,... | collective-permute-start | bytes 589832 | tf_op jit(solution)/shard_map/ppermute | solution.py:850
  55.4 14.0 %collective-permute-start.14 = (bf16[512,192]{1,0:T(8,128)(2,1)}, bf16[512,192]{1,0:T(8,128)(2,1)S(1)}, u32[]{:S(2)}, u32[]{:S(2)}) collective-permute-start(bf16[512,192]{1,0:T(8,128)(2,1)} %get-tuple-element.158), channel_id=1, source_target_pairs={{0,3},{1,2},{2,1},{3,0},{4,7},{5,6},{6,5},{7,4},{8,11},{9,10},{10,... | collective-permute-start | bytes 589832 | tf_op jit(solution)/shard_map/ppermute | solution.py:850
  69.4 15.5 %copy-start.25 = (bf16[512,192]{1,0:T(8,128)(2,1)S(1)}, bf16[512,192]{1,0:T(8,128)(2,1)}, u32[]{:S(2)}) copy-start(bf16[512,192]{1,0:T(8,128)(2,1)} %get-tuple-element.179) | copy-start | bytes 589828
  69.5 16.3 %copy-start.24 = (bf16[512,192]{1,0:T(8,128)(2,1)S(1)}, bf16[512,192]{1,0:T(8,128)(2,1)}, u32[]{:S(2)}) copy-start(bf16[512,192]{1,0:T(8,128)(2,1)} %get-tuple-element.180) | copy-start | bytes 589828
  69.5 16.8 %copy-start.23 = (bf16[512,192]{1,0:T(8,128)(2,1)S(1)}, bf16[512,192]{1,0:T(8,128)(2,1)}, u32[]{:S(2)}) copy-start(bf16[512,192]{1,0:T(8,128)(2,1)} %get-tuple-element.181) | copy-start | bytes 589828
  69.5 15.4 %collective-permute-start.15 = (bf16[512,192]{1,0:T(8,128)(2,1)S(1)}, bf16[512,192]{1,0:T(8,128)(2,1)S(1)}, u32[]{:S(2)}, u32[]{:S(2)}) collective-permute-start(bf16[512,192]{1,0:T(8,128)(2,1)S(1)} %copy-done.28), channel_id=1, source_target_pairs={{0,1},{1,0},{2,3},{3,2},{4,5},{5,4},{6,7},{7,6},{8,9},{9,8},{10,11... | collective-permute-start | bytes 589832 | tf_op jit(solution)/shard_map/ppermute | solution.py:850
  70.2 14.7 %collective-permute-start.16 = (bf16[512,192]{1,0:T(8,128)(2,1)S(1)}, bf16[512,192]{1,0:T(8,128)(2,1)S(1)}, u32[]{:S(2)}, u32[]{:S(2)}) collective-permute-start(bf16[512,192]{1,0:T(8,128)(2,1)S(1)} %copy-done.27), channel_id=1, source_target_pairs={{0,2},{1,3},{2,0},{3,1},{4,6},{5,7},{6,4},{7,5},{8,10},{9,11},{10,... | collective-permute-start | bytes 589832 | tf_op jit(solution)/shard_map/ppermute | solution.py:850
  70.8 14.2 %collective-permute-start.17 = (bf16[512,192]{1,0:T(8,128)(2,1)S(1)}, bf16[512,192]{1,0:T(8,128)(2,1)S(1)}, u32[]{:S(2)}, u32[]{:S(2)}) collective-permute-start(bf16[512,192]{1,0:T(8,128)(2,1)S(1)} %copy-done.26), channel_id=1, source_target_pairs={{0,3},{1,2},{2,1},{3,0},{4,7},{5,6},{6,5},{7,4},{8,11},{9,10},{10,... | collective-permute-start | bytes 589832 | tf_op jit(solution)/shard_map/ppermute | solution.py:850
  84.9 16.1 %collective-permute-start.18 = (bf16[512,192]{1,0:T(8,128)(2,1)S(1)}, bf16[512,192]{1,0:T(8,128)(2,1)S(1)}, u32[]{:S(2)}, u32[]{:S(2)}) collective-permute-start(bf16[512,192]{1,0:T(8,128)(2,1)S(1)} %copy-done.25), channel_id=1, source_target_pairs={{0,1},{1,0},{2,3},{3,2},{4,5},{5,4},{6,7},{7,6},{8,9},{9,8},{10,11... | collective-permute-start | bytes 589832 | tf_op jit(solution)/shard_map/ppermute | solution.py:850
  85.7 15.3 %collective-permute-start.19 = (bf16[512,192]{1,0:T(8,128)(2,1)S(1)}, bf16[512,192]{1,0:T(8,128)(2,1)S(1)}, u32[]{:S(2)}, u32[]{:S(2)}) collective-permute-start(bf16[512,192]{1,0:T(8,128)(2,1)S(1)} %copy-done.24), channel_id=1, source_target_pairs={{0,2},{1,3},{2,0},{3,1},{4,6},{5,7},{6,4},{7,5},{8,10},{9,11},{10,... | collective-permute-start | bytes 589832 | tf_op jit(solution)/shard_map/ppermute | solution.py:850
  86.2 14.8 %collective-permute-start.20 = (bf16[512,192]{1,0:T(8,128)(2,1)S(1)}, bf16[512,192]{1,0:T(8,128)(2,1)S(1)}, u32[]{:S(2)}, u32[]{:S(2)}) collective-permute-start(bf16[512,192]{1,0:T(8,128)(2,1)S(1)} %copy-done.23), channel_id=1, source_target_pairs={{0,3},{1,2},{2,1},{3,0},{4,7},{5,6},{6,5},{7,4},{8,11},{9,10},{10,... | collective-permute-start | bytes 589832 | tf_op jit(solution)/shard_map/ppermute | solution.py:850
  87.2 27.7 %collective-permute-start.10 = (bf16[784,768]{1,0:T(8,128)(2,1)}, bf16[784,768]{1,0:T(8,128)(2,1)S(1)}, u32[]{:S(2)}, u32[]{:S(2)}) collective-permute-start(bf16[784,768]{1,0:T(8,128)(2,1)} %collective-permute-done.3.refs_13_), channel_id=1, source_target_pairs={{0,1},{1,0},{2,3},{3,2},{4,5},{5,4},{6,7},{7,6},{8,9},{9,8},{10,11... | collective-permute-start | bytes 3612680 | tf_op jit(solution)/shard_map/ppermute | solution.py:850
  101.1 13.8 %collective-permute-start.21 = (bf16[784,768]{1,0:T(8,128)(2,1)S(1)}, bf16[784,768]{1,0:T(8,128)(2,1)S(1)}, u32[]{:S(2)}, u32[]{:S(2)}) collective-permute-start(bf16[784,768]{1,0:T(8,128)(2,1)S(1)} %collective-permute-done.11.refs_15_), channel_id=1, source_target_pairs={{0,1},{1,0},{2,3},{3,2},{4,5},{5,4},{6,7},{7,6},{8,9},{9,8},{10,11... | collective-permute-start | bytes 3612680 | tf_op jit(solution)/shard_map/ppermute | solution.py:850
  190.2 1.5 collective-permute-start.22
  192.5 4.1 %collective-permute-start.23 = (f32[104,128]{1,0:T(8,128)S(1)}, f32[104,128]{1,0:T(8,128)S(1)}, u32[]{:S(2)}, u32[]{:S(2)}) collective-permute-start(f32[104,128]{1,0:T(8,128)S(1)} %add.19), channel_id=1, source_target_pairs={{0,2},{1,3},{2,0},{3,1},{4,6},{5,7},{6,4},{7,5},{8,10},{9,11},{10,... | collective-permute-start | bytes 159752 | tf_op jit(solution)/shard_map/ppermute | solution.py:850
  196.6 4.2 %collective-permute-start.24 = (f32[104,128]{1,0:T(8,128)S(1)}, f32[104,128]{1,0:T(8,128)S(1)}, u32[]{:S(2)}, u32[]{:S(2)}) collective-permute-start(f32[104,128]{1,0:T(8,128)S(1)} %add.20), channel_id=1, source_target_pairs={{0,4},{4,0},{8,12},{12,8},{16,20},{20,16},{24,28},{28,24},{1,5},{5... | collective-permute-start | bytes 159752 | tf_op jit(solution)/shard_map/ppermute | solution.py:850
  200.8 4.2 %collective-permute-start.25 = (f32[104,128]{1,0:T(8,128)S(1)}, f32[104,128]{1,0:T(8,128)S(1)}, u32[]{:S(2)}, u32[]{:S(2)}) collective-permute-start(f32[104,128]{1,0:T(8,128)S(1)} %add.21), channel_id=1, source_target_pairs={{0,8},{4,12},{8,0},{12,4},{16,24},{20,28},{24,16},{28,20},{1,9},{5... | collective-permute-start | bytes 159752 | tf_op jit(solution)/shard_map/ppermute | solution.py:850
  205.1 5.2 %collective-permute-start.26 = (f32[104,128]{1,0:T(8,128)S(1)}, f32[104,128]{1,0:T(8,128)S(1)}, u32[]{:S(2)}, u32[]{:S(2)}) collective-permute-start(f32[104,128]{1,0:T(8,128)S(1)} %add.22.acc_ref), channel_id=1, source_target_pairs={{0,16},{4,20},{8,24},{12,28},{16,0},{20,4},{24,8},{28,12},{1,17},{... | collective-permute-start | bytes 159752 | tf_op jit(solution)/shard_map/ppermute | solution.py:850
  (24 other events, 122.4 us)
